TPU v7x, 32 devices: a whole 2x2x4 slice. The times are simulated.
32 devices in a mesh: cmp: 4 (over x, core), lmk: 8 (over z, y).
Axes of the slice: x: 2, y: 2, z: 4, core: 2. Of those that a mesh axis runs over, the one named last changes fastest.
Arguments:
- compounds: bfloat16 [32768, 512], P(('cmp', 'lmk')), may hold values from -6 to 6
- targets: bfloat16 [32768, 128], P(('cmp', 'lmk')), may hold values from -6 to 6
- cluster_lists: int32 [32768, 4], P(('cmp', 'lmk')), may hold values from 0 to 127, as said below
- landmarks: bfloat16 [128, 256, 512], P('lmk'), may hold values from -6 to 6
- neighbours: int32 [128, 8], replicated, may hold values from 0 to 127, as said below
Outputs:
- normal_blocks: float32 [256, 128, 8, 256], P('cmp', 'lmk')
- right_sides: float32 [256, 128, 128], P('cmp', 'lmk')
Inputs may be any that keep to these rules, and one draw needn't show every extreme that they name: `cluster_lists`: each compound lists 4 different clusters, each within 7 clusters of its first entry, counted cyclically modulo 128. In each aligned block of 1024 rows (the compounds of one device) no cluster is listed by more than 64 rows, and in every block some cluster is listed by exactly 64. neighbours[a, 0] = a; the entries of a row are distinct; every row has the same offsets, neighbours[a, j] = (a + neighbours[0, j]) modulo 128, and each entry differs from a by at most 8 clusters, counted cyclically.
All inputs are finite; a program needn't handle non-finite values.
Results may differ from a plain program's by a relative error of at most 0.0048.
Values may be sent and summed in bfloat16 or wider, within the bound.
A program may use at most 192 MiB of HBM per device.

v0:
```python
import math

import jax
import jax.numpy as jnp
from jax import lax
from jax.sharding import PartitionSpec as P


def padded(block, sides, width):
    for axis, dim in sides:
        count = lax.axis_size(axis)
        forward = [(i, i + 1) for i in range(count - 1)]
        forward.append((count - 1, 0))
        backward = [(target, source) for source, target in forward]
        low = lax.ppermute(
            lax.slice_in_dim(block, block.shape[dim] - width, None, axis=dim), axis, forward
        )
        high = lax.ppermute(lax.slice_in_dim(block, 0, width, axis=dim), axis, backward)
        block = jnp.concatenate([low, block, high], axis=dim)
    return block


def normalize(data):
    wide = data.astype(jnp.float32)
    return (wide * lax.rsqrt(jnp.sum(wide * wide, axis=-1, keepdims=True) + 1e-06)).astype(
        jnp.bfloat16
    )


def pack_slots(compounds, targets, cluster_lists, neighbours, position_of, slot_cap):
    unit_rows = normalize(compounds)
    picks = cluster_lists.shape[1]
    flat_lists = cluster_lists.reshape(-1)
    listing_count = flat_lists.shape[0]
    order = jnp.argsort(flat_lists, stable=True)
    ordered = flat_lists[order]
    first_seen = jnp.searchsorted(ordered, ordered, side="left")
    rank_sorted = jnp.arange(listing_count, dtype=jnp.int32) - first_seen
    rank = jnp.zeros((listing_count,), jnp.int32).at[order].set(rank_sorted)
    own_lists = jnp.repeat(cluster_lists, picks, axis=0)
    near = neighbours[flat_lists]
    flags = jnp.any(near[:, :, None] == own_lists[:, None, :], axis=2).astype(jnp.bfloat16)
    slot = position_of(flat_lists) * slot_cap + rank
    total_slots = neighbours.shape[0] * slot_cap
    row_buffer = (
        jnp.zeros((total_slots, unit_rows.shape[1]), jnp.bfloat16)
        .at[slot]
        .set(jnp.repeat(unit_rows, picks, axis=0))
    )
    aim_buffer = (
        jnp.zeros((total_slots, targets.shape[1]), jnp.bfloat16)
        .at[slot]
        .set(jnp.repeat(targets, picks, axis=0))
    )
    flag_buffer = jnp.zeros((total_slots, near.shape[1]), jnp.bfloat16).at[slot].set(flags)
    return (row_buffer, aim_buffer, flag_buffer)


def owner_tiles(rows, aims, flags, cluster_rows, extended, first_row, cluster_count):
    kernel_scale = 0.75 * math.sqrt(rows.shape[2])
    mark_count = extended.shape[1]
    width = extended.shape[2]
    owned = rows.shape[0]
    flat_marks = extended.reshape(-1, width)
    kern_parts = []
    for near_slot in range(cluster_rows.shape[1]):
        spot = jnp.mod(cluster_rows[0, near_slot] - first_row, cluster_count)
        marks = lax.dynamic_slice_in_dim(flat_marks, spot * mark_count, owned * mark_count, 0)
        marks = marks.reshape(owned, mark_count, width)
        scores = lax.dot_general(
            rows, marks, (((2,), (2,)), ((0,), (0,))), preferred_element_type=jnp.float32
        )
        flag_column = flags[:, :, near_slot : near_slot + 1].astype(jnp.float32)
        kern = (jnp.exp(kernel_scale * scores - 4.0) * flag_column).astype(jnp.bfloat16)
        kern_parts.append(kern)
    tiles = jnp.concatenate(kern_parts + [aims], axis=2)
    return (kern_parts[0], tiles)


def on_device(compounds, targets, cluster_lists, landmarks, neighbours):
    lmk_count = lax.axis_size("lmk")
    my_lmk = lax.axis_index("lmk")
    local_clusters = landmarks.shape[0]
    rim_width = local_clusters // 2
    mark_count = landmarks.shape[1]
    width = compounds.shape[1]
    aim_width = targets.shape[1]
    near_count = neighbours.shape[1]
    cluster_count = neighbours.shape[0]
    slot_cap = cluster_lists.shape[1] * (2 * compounds.shape[0] // cluster_count)
    unit_marks = normalize(landmarks)
    extended = padded(unit_marks, (("lmk", 0),), rim_width)
    first_row = my_lmk * local_clusters - rim_width
    row_buffer, aim_buffer, flag_buffer = pack_slots(
        compounds, targets, cluster_lists, neighbours, lambda cluster: cluster, slot_cap
    )
    row_buffer = row_buffer.reshape(lmk_count, local_clusters, slot_cap, width)
    aim_buffer = aim_buffer.reshape(lmk_count, local_clusters, slot_cap, aim_width)
    flag_buffer = flag_buffer.reshape(lmk_count, local_clusters, slot_cap, near_count)
    got_rows, got_aims, got_flags = (
        lax.all_to_all(row_buffer, "lmk", split_axis=0, concat_axis=2, tiled=True),
        lax.all_to_all(aim_buffer, "lmk", split_axis=0, concat_axis=2, tiled=True),
        lax.all_to_all(flag_buffer, "lmk", split_axis=0, concat_axis=2, tiled=True),
    )
    cluster_rows = lax.dynamic_slice_in_dim(neighbours, my_lmk * local_clusters, local_clusters, 0)
    first_cols, tiles = owner_tiles(
        got_rows[0], got_aims[0], got_flags[0], cluster_rows, extended, first_row, cluster_count
    )
    shard = lax.psum_scatter(
        jnp.einsum("krm,krc->mkc", first_cols, tiles, preferred_element_type=jnp.float32),
        "cmp",
        scatter_dimension=0,
        tiled=True,
    )
    normal_blocks = shard[:, :, : near_count * mark_count].reshape(
        shard.shape[0], local_clusters, near_count, mark_count
    )
    right_sides = shard[:, :, near_count * mark_count :]
    return (normal_blocks, right_sides)


def solution(mesh):
    placed = (
        P(("cmp", "lmk"), None),
        P(("cmp", "lmk"), None),
        P(("cmp", "lmk"), None),
        P("lmk", None, None),
        P(),
    )
    return jax.shard_map(
        on_device,
        mesh=mesh,
        in_specs=placed,
        out_specs=(P("cmp", "lmk", None, None), P("cmp", "lmk", None)),
        check_vma=False,
    )
```

profile of v0, /device:TPU:0, one launch (start us, length us, event | category | flops | bytes accessed | tf_op | source)
XLA Modules:
  0.0 1146.5 jit_solution(15741669450090546345)
XLA Ops:
  14.6 23.0 %gather_fusion.1 = s32[4096]{0:T(1024)S(1)} fusion(s32[4096]{0:T(1024)S(1)} %reshape.99, s32[4096]{0:T(1024)S(1)} %get-tuple-element.121), kind=kCustom, calls=%fused_computation.1 | custom fusion | bytes 49152 | tf_op jit(solution)/shard_map/gather | solution.py:36
  37.6 300.6 %while.25 = (s32[]{:T(128)}, u32[4096]{0:T(1024)S(1)}, u32[4096]{0:T(1024)S(1)}, s32[4096]{0:T(1024)S(1)}, s32[]{:T(128)}, /*index=5*/s32[]{:T(128)}, s32[]{}) while((s32[]{:T(128)}, u32[4096]{0:T(1024)S(1)}, u32[4096]{0:T(1024)S(1)}, s32[4096]{0:T(1024)S(1)}, s32[]{:T(128)}, /*index=5*/s32[]{:T(128)}, s32[]{}) %tuple.68), condition=%wide.region_2.0_spmd.clone, body=%wide.region_1.0_spmd.clone.sunk | while | flops 77828 | bytes 270437 | solution.py:37
  37.6 23.0 %gather_fusion = s32[4096]{0:T(1024)S(1)} fusion(s32[4096]{0:T(1024)S(1)} %get-tuple-element.180, u32[4096]{0:T(1024)S(1)} %broadcast_clamp_fusion.4), kind=kCustom, calls=%fused_computation.clone.clone.1 | custom fusion | bytes 49152 | tf_op jit(solution)/shard_map/jit(searchsorted)/jit(_searchsorted_scan_impl)/vmap(jit(_searchsorted_scan_impl))/while/body/eval_jaxpr/gather | solution.py:37
  60.8 23.0 %gather_fusion = s32[4096]{0:T(1024)S(1)} fusion(s32[4096]{0:T(1024)S(1)} %get-tuple-element.180, u32[4096]{0:T(1024)S(1)} %broadcast_clamp_fusion.4), kind=kCustom, calls=%fused_computation.clone.clone.1 | custom fusion | bytes 49152 | tf_op jit(solution)/shard_map/jit(searchsorted)/jit(_searchsorted_scan_impl)/vmap(jit(_searchsorted_scan_impl))/while/body/eval_jaxpr/gather | solution.py:37
  83.9 23.0 %gather_fusion = s32[4096]{0:T(1024)S(1)} fusion(s32[4096]{0:T(1024)S(1)} %get-tuple-element.180, u32[4096]{0:T(1024)S(1)} %broadcast_clamp_fusion.4), kind=kCustom, calls=%fused_computation.clone.clone.1 | custom fusion | bytes 49152 | tf_op jit(solution)/shard_map/jit(searchsorted)/jit(_searchsorted_scan_impl)/vmap(jit(_searchsorted_scan_impl))/while/body/eval_jaxpr/gather | solution.py:37
  107.0 23.0 %gather_fusion = s32[4096]{0:T(1024)S(1)} fusion(s32[4096]{0:T(1024)S(1)} %get-tuple-element.180, u32[4096]{0:T(1024)S(1)} %broadcast_clamp_fusion.4), kind=kCustom, calls=%fused_computation.clone.clone.1 | custom fusion | bytes 49152 | tf_op jit(solution)/shard_map/jit(searchsorted)/jit(_searchsorted_scan_impl)/vmap(jit(_searchsorted_scan_impl))/while/body/eval_jaxpr/gather | solution.py:37
  130.2 23.0 %gather_fusion = s32[4096]{0:T(1024)S(1)} fusion(s32[4096]{0:T(1024)S(1)} %get-tuple-element.180, u32[4096]{0:T(1024)S(1)} %broadcast_clamp_fusion.4), kind=kCustom, calls=%fused_computation.clone.clone.1 | custom fusion | bytes 49152 | tf_op jit(solution)/shard_map/jit(searchsorted)/jit(_searchsorted_scan_impl)/vmap(jit(_searchsorted_scan_impl))/while/body/eval_jaxpr/gather | solution.py:37
  153.3 23.0 %gather_fusion = s32[4096]{0:T(1024)S(1)} fusion(s32[4096]{0:T(1024)S(1)} %get-tuple-element.180, u32[4096]{0:T(1024)S(1)} %broadcast_clamp_fusion.4), kind=kCustom, calls=%fused_computation.clone.clone.1 | custom fusion | bytes 49152 | tf_op jit(solution)/shard_map/jit(searchsorted)/jit(_searchsorted_scan_impl)/vmap(jit(_searchsorted_scan_impl))/while/body/eval_jaxpr/gather | solution.py:37
  176.4 23.0 %gather_fusion = s32[4096]{0:T(1024)S(1)} fusion(s32[4096]{0:T(1024)S(1)} %get-tuple-element.180, u32[4096]{0:T(1024)S(1)} %broadcast_clamp_fusion.4), kind=kCustom, calls=%fused_computation.clone.clone.1 | custom fusion | bytes 49152 | tf_op jit(solution)/shard_map/jit(searchsorted)/jit(_searchsorted_scan_impl)/vmap(jit(_searchsorted_scan_impl))/while/body/eval_jaxpr/gather | solution.py:37
  199.5 23.0 %gather_fusion = s32[4096]{0:T(1024)S(1)} fusion(s32[4096]{0:T(1024)S(1)} %get-tuple-element.180, u32[4096]{0:T(1024)S(1)} %broadcast_clamp_fusion.4), kind=kCustom, calls=%fused_computation.clone.clone.1 | custom fusion | bytes 49152 | tf_op jit(solution)/shard_map/jit(searchsorted)/jit(_searchsorted_scan_impl)/vmap(jit(_searchsorted_scan_impl))/while/body/eval_jaxpr/gather | solution.py:37
  222.7 23.0 %gather_fusion = s32[4096]{0:T(1024)S(1)} fusion(s32[4096]{0:T(1024)S(1)} %get-tuple-element.180, u32[4096]{0:T(1024)S(1)} %broadcast_clamp_fusion.4), kind=kCustom, calls=%fused_computation.clone.clone.1 | custom fusion | bytes 49152 | tf_op jit(solution)/shard_map/jit(searchsorted)/jit(_searchsorted_scan_impl)/vmap(jit(_searchsorted_scan_impl))/while/body/eval_jaxpr/gather | solution.py:37
  245.8 23.0 %gather_fusion = s32[4096]{0:T(1024)S(1)} fusion(s32[4096]{0:T(1024)S(1)} %get-tuple-element.180, u32[4096]{0:T(1024)S(1)} %broadcast_clamp_fusion.4), kind=kCustom, calls=%fused_computation.clone.clone.1 | custom fusion | bytes 49152 | tf_op jit(solution)/shard_map/jit(searchsorted)/jit(_searchsorted_scan_impl)/vmap(jit(_searchsorted_scan_impl))/while/body/eval_jaxpr/gather | solution.py:37
  268.9 23.0 %gather_fusion = s32[4096]{0:T(1024)S(1)} fusion(s32[4096]{0:T(1024)S(1)} %get-tuple-element.180, u32[4096]{0:T(1024)S(1)} %broadcast_clamp_fusion.4), kind=kCustom, calls=%fused_computation.clone.clone.1 | custom fusion | bytes 49152 | tf_op jit(solution)/shard_map/jit(searchsorted)/jit(_searchsorted_scan_impl)/vmap(jit(_searchsorted_scan_impl))/while/body/eval_jaxpr/gather | solution.py:37
  292.0 23.0 %gather_fusion = s32[4096]{0:T(1024)S(1)} fusion(s32[4096]{0:T(1024)S(1)} %get-tuple-element.180, u32[4096]{0:T(1024)S(1)} %broadcast_clamp_fusion.4), kind=kCustom, calls=%fused_computation.clone.clone.1 | custom fusion | bytes 49152 | tf_op jit(solution)/shard_map/jit(searchsorted)/jit(_searchsorted_scan_impl)/vmap(jit(_searchsorted_scan_impl))/while/body/eval_jaxpr/gather | solution.py:37
  315.2 23.0 %gather_fusion = s32[4096]{0:T(1024)S(1)} fusion(s32[4096]{0:T(1024)S(1)} %get-tuple-element.180, u32[4096]{0:T(1024)S(1)} %broadcast_clamp_fusion.4), kind=kCustom, calls=%fused_computation.clone.clone.1 | custom fusion | bytes 49152 | tf_op jit(solution)/shard_map/jit(searchsorted)/jit(_searchsorted_scan_impl)/vmap(jit(_searchsorted_scan_impl))/while/body/eval_jaxpr/gather | solution.py:37
  338.3 15.5 %scatter_custom_fusion = s32[4096]{0:T(1024)S(1)} fusion(s32[4096]{0:T(1024)S(1)} %get-tuple-element.122, s32[4096]{0:T(1024)S(1)} %convert_subtract_fusion, s32[]{:T(128)} %constant.102.clone.1), kind=kCustom, calls=%fused_computation.68 | custom fusion | bytes 16388 | tf_op jit(solution)/shard_map/scatter | solution.py:39
  391.5 12.4 %scatter_custom_fusion.3 = bf16[8192,128]{1,0:T(8,128)(2,1)} fusion(s32[4096]{0:T(1024)S(1)} %compare_select_fusion.1, bf16[4096,128]{1,0:T(8,128)(2,1)S(1)} %bitcast.117, bf16[]{:T(256)} %constant.100.clone.1), kind=kCustom, calls=%fused_computation.38 | custom fusion | bytes 2097154 | tf_op jit(solution)/shard_map/scatter | solution.py:53
  420.5 23.6 %scatter_custom_fusion.1 = bf16[8192,512]{1,0:T(8,128)(2,1)} fusion(s32[4096]{0:T(1024)S(1)} %compare_select_fusion.1, bf16[4096,512]{1,0:T(8,128)(2,1)} %reshape.160, bf16[]{:T(256)} %constant.100.clone.1), kind=kCustom, calls=%fused_computation.32 | custom fusion | bytes 8389120 | tf_op jit(solution)/shard_map/scatter | solution.py:48
  444.1 13.5 %all-to-all-done.2 = bf16[8,16,64,128]{3,2,1,0:T(8,128)(2,1)S(1)} async-done(((bf16[8,16,64,128]{3,2,1,0:T(8,128)(2,1)}), bf16[8,16,64,128]{3,2,1,0:T(8,128)(2,1)S(1)}, u32[]{:S(2)}, u32[]{:S(2)}) %all-to-all-start.2) | async-done | bytes 2097184 | tf_op jit(solution)/shard_map/all_to_all | solution.py:102
  484.0 162.6 %collective-permute-done = bf16[8,256,512]{2,1,0:T(8,128)(2,1)} collective-permute-done((bf16[8,256,512]{2,1,0:T(8,128)(2,1)}, bf16[8,256,512]{2,1,0:T(8,128)(2,1)}, u32[]{:S(2)}, u32[]{:S(2)}) %collective-permute-start) | collective-permute-done | bytes 2097184 | tf_op jit(solution)/shard_map/ppermute | solution.py:15
  653.7 23.3 %constant_dynamic-slice_fusion = (bf16[4096,512]{1,0:T(8,128)(2,1)}, bf16[4096,512]{1,0:T(8,128)(2,1)}, bf16[4096,512]{1,0:T(8,128)(2,1)}, bf16[4096,512]{1,0:T(...) fusion(bf16[8192,512]{1,0:T(8,128)(2,1)} %bitcast.91, ...), kind=kLoop, calls=%fused_computation.71 | loop fusion | bytes 67108896 | tf_op jit(solution)/shard_map/dynamic_slice | solution.py:68
  775.3 25.5 %convolution_bitcast_fusion = f32[256,16,2176]{0,2,1:T(8,128)} fusion(bf16[16,512,2176]{1,2,0:T(8,128)(2,1)} %constant_dynamic-update-slice_fusion, bf16[16,512,256]{1,2,0:T(8,128)(2,1)} %get-tuple-element.132), kind=kOutput, calls=%fused_computation.11 | convolution fusion | flops 9126805504 | bytes 75497472 | tf_op jit(solution)/shard_map/krm,krc->mkc/dot_general | solution.py:110
  800.8 37.3 %copy.71 = f32[256,16,2176]{2,1,0:T(8,128)} copy(f32[256,16,2176]{0,2,1:T(8,128)} %convolution_bitcast_fusion) | data formatting | bytes 71303168 | tf_op jit(solution)/shard_map/krm,krc->mkc/transpose | solution.py:110
  838.1 289.2 %reduce-scatter.2.cloned.1.call-done = f32[64,16,2176]{2,1,0:T(8,128)} async-done(((f32[256,16,2176]{2,1,0:T(8,128)}), f32[64,16,2176]{2,1,0:T(8,128)}) %reduce-scatter.2.cloned.1.call-update) | async-done | bytes 8912912 | tf_op jit(solution)/shard_map/reduce_scatter | solution.py:109
  (141 shorter events, 200.4 us)
Async XLA Ops:
  37.6 316.2 %copy-start.3 = (s32[128,8]{0,1:T(8,128)S(1)}, s32[128,8]{0,1:T(8,128)}, u32[]{:S(2)}) copy-start(s32[128,8]{0,1:T(8,128)} %param.11) | copy-start | bytes 12292
  353.9 11.4 copy-start.2
  365.9 44.0 %copy-start.1 = (bf16[1024,512]{1,0:T(8,128)(2,1)S(1)}, bf16[1024,512]{1,0:T(8,128)(2,1)}, u32[]{:S(2)}) copy-start(bf16[1024,512]{1,0:T(8,128)(2,1)} %param.7) | copy-start | bytes 3145732
  382.7 21.2 %all-to-all-start.1 = ((bf16[8,2,4096]{2,1,0:T(2,128)(2,1)}), bf16[8,2,4096]{2,1,0:T(2,128)(2,1)S(1)}, u32[]{:S(2)}, u32[]{:S(2)}) async-start(bf16[8,2,4096]{2,1,0:T(2,128)(2,1)} %reshape.197), calls=%async_computation.1 | async-start | bytes 262144 | tf_op jit(solution)/shard_map/all_to_all | solution.py:103
  403.9 53.7 %all-to-all-start.2 = ((bf16[8,16,64,128]{3,2,1,0:T(8,128)(2,1)}), bf16[8,16,64,128]{3,2,1,0:T(8,128)(2,1)S(1)}, u32[]{:S(2)}, u32[]{:S(2)}) async-start(bf16[8,16,64,128]{3,2,1,0:T(8,128)(2,1)} %bitcast.107), calls=%async_computation.2 | async-start | bytes 4194304 | tf_op jit(solution)/shard_map/all_to_all | solution.py:102
  457.6 232.6 %all-to-all-start = ((bf16[8,16,64,512]{3,2,1,0:T(8,128)(2,1)}), bf16[8,16,64,512]{3,2,1,0:T(8,128)(2,1)}, u32[]{:S(2)}, u32[]{:S(2)}) async-start(bf16[8,16,64,512]{3,2,1,0:T(8,128)(2,1)} %bitcast.92), calls=%async_computation | async-start | bytes 16777216 | tf_op jit(solution)/shard_map/all_to_all | solution.py:101
  462.6 664.8 %reduce-scatter.2.cloned.1.call-start = ((), (), s32[]{:S(2)}) async-start(), calls=%async_computation.4 | async-start | bytes 44564480 | tf_op jit(solution)/shard_map/reduce_scatter | solution.py:109
  468.5 1.9 copy-start
  472.6 174.0 %collective-permute-start = (bf16[8,256,512]{2,1,0:T(8,128)(2,1)}, bf16[8,256,512]{2,1,0:T(8,128)(2,1)}, u32[]{:S(2)}, u32[]{:S(2)}) collective-permute-start(bf16[8,256,512]{2,1,0:T(8,128)(2,1)} %get-tuple-element.111), channel_id=1, source_target_pairs={{0,1},{1,2},{2,3},{3,4},{4,5},{5,6},{6,7},{7,0},{8,9},{9,10},{10,1... | collective-permute-start | bytes 6291464 | tf_op jit(solution)/shard_map/ppermute | solution.py:15
  474.5 172.1 %collective-permute-start.1 = (bf16[8,256,512]{2,1,0:T(8,128)(2,1)}, bf16[8,256,512]{2,1,0:T(8,128)(2,1)}, u32[]{:S(2)}, u32[]{:S(2)}) collective-permute-start(bf16[8,256,512]{2,1,0:T(8,128)(2,1)} %get-tuple-element.112), channel_id=1, source_target_pairs={{1,0},{2,1},{3,2},{4,3},{5,4},{6,5},{7,6},{0,7},{9,8},{10,9},{11,1... | collective-permute-start | bytes 6291464 | tf_op jit(solution)/shard_map/ppermute | solution.py:18
  1127.3 3.4 slice-start.3
  1127.3 11.0 slice-start
  1127.3 11.0 slice-start.1
  1130.7 7.6 slice-start.2
Sparse Core Ops, SparseCore 0:
  838.3 289.0 reduce-scatter.1
where the time goes:
time: 1160 us; the launch traced here: 1150 us
  local copies, waits for them, and re-layouts  516 us (44%)
  waiting for transfers between devices  465 us (40%)
  matrix products  101 us (9%)
  starting transfers between devices  23.3 us (2%)
  other arithmetic  20 us (2%)
  between operations  19.9 us (2%)
    gather x13, local copies, waits for them, and re-layouts, pack_slots(): first_seen = jnp.searchsorted(ordered, ordered, side='left')  299 us
    reduce_scatter x1, waiting for transfers between devices, on_device(): lax.psum_scatter(jnp.einsum('krm,krc->mkc', first_cols, tiles, preferred_...  289 us
    ppermute x1, waiting for transfers between devices, padded(): lax.ppermute(lax.slice_in_dim(block, block.shape[dim] - width, None, axis...  163 us
    dot_general x8, matrix products, owner_tiles(): lax.dot_general(rows, marks, (((2,), (2,)), ((0,), (0,))), preferred_elem...  75.7 us
    transpose x1, local copies, waits for them, and re-layouts, on_device(): jnp.einsum('krm,krc->mkc', first_cols, tiles, preferred_element_type=jnp....  37.3 us
    dot_general x1, matrix products, on_device(): jnp.einsum('krm,krc->mkc', first_cols, tiles, preferred_element_type=jnp....  25.5 us
    scatter x1, local copies, waits for them, and re-layouts, pack_slots(): row_buffer = jnp.zeros((total_slots, unit_rows.shape[1]), jnp.bfloat16).a...  23.6 us
    dynamic_slice x1, local copies, waits for them, and re-layouts, owner_tiles(): lax.dynamic_slice_in_dim(flat_marks, spot * mark_count, owned * mark_coun...  23.3 us
  transfers between devices with their start and end apart: 6, of which 3 were waited for; matrix products, arithmetic and copies ran while one was open for 9% of the time, Pallas kernels for 0%

commit v1 on v0

v1 whole, which is shorter than its diff:
```python
import functools
import math

import jax
import jax.numpy as jnp
from jax import lax
from jax.experimental import pallas as pl
from jax.experimental.pallas import tpu as pltpu
from jax.sharding import PartitionSpec as P

LIFT = 8.0
FLAG_LANES = 128
CHUNKS = 4


def normalize(data):
    wide = data.astype(jnp.float32)
    return (wide * lax.rsqrt(jnp.sum(wide * wide, axis=-1, keepdims=True) + 1e-06)).astype(
        jnp.bfloat16
    )


def dispatch_kernel(
    cluster_count, first_ref, lists_ref, rows_ref, out_ref, rank_ref, hit_ref
):
    sources, picks, count = lists_ref.shape
    owned, _, cap, _ = out_ref.shape
    width = rows_ref.shape[2] - FLAG_LANES
    rim = owned // 2
    extended = owned + 2 * rim
    step = pl.program_id(0)

    @pl.when(step == 0)
    def _():
        first = first_ref[0]
        index = lax.broadcasted_iota(jnp.int32, (FLAG_LANES, count), 0)
        ident = index + (first - rim + cluster_count)
        ident = jnp.where(ident >= cluster_count, ident - cluster_count, ident)
        ident = jnp.where(ident >= cluster_count, ident - cluster_count, ident)
        ident = jnp.where(index < extended, ident, -1)
        for source in range(sources):
            hit = lists_ref[source, 0:1, :] == ident
            for pick in range(1, picks):
                hit = hit | (lists_ref[source, pick : pick + 1, :] == ident)
            hit_ref[source] = jnp.where(hit, 1.0, 0.0).astype(jnp.bfloat16)
        before = lax.broadcasted_iota(jnp.int32, (count, count), 0) < lax.broadcasted_iota(
            jnp.int32, (count, count), 1
        )
        before = jnp.where(before, 1.0, 0.0).astype(jnp.bfloat16)
        own = hit_ref[:, rim : rim + owned, :].reshape(sources * owned, count)
        rank = jnp.dot(own, before, preferred_element_type=jnp.float32)
        rank = jnp.where(own.astype(jnp.float32) > 0.5, rank, -1.0)
        rank_ref[...] = rank.astype(jnp.int32).reshape(sources, owned, count)

    group = max(1, 256 // cap)
    slot = lax.broadcasted_iota(jnp.int32, (cap, count), 0)
    for start in range(0, owned, group):
        picked = jnp.concatenate(
            [
                jnp.where(rank_ref[step, pl.ds(start + k, 1), :] == slot, 1.0, 0.0).astype(
                    jnp.bfloat16
                )
                for k in range(group)
            ],
            axis=0,
        )
        moved = jnp.dot(picked, rows_ref[0], preferred_element_type=jnp.float32)
        flags = lax.dot_general(
            picked, hit_ref[step], (((1,), (1,)), ((), ())), preferred_element_type=jnp.float32
        )
        moved = moved.astype(jnp.bfloat16).reshape(group, cap, moved.shape[1])
        flags = flags.astype(jnp.bfloat16).reshape(group, cap, FLAG_LANES)
        out_ref[start : start + group, 0, :, :width] = moved[:, :, :width]
        out_ref[start : start + group, 0, :, width : width + FLAG_LANES] = flags
        out_ref[start : start + group, 0, :, width + FLAG_LANES :] = moved[:, :, width:]


def dispatch(first, lists, rows, owned, cap, cluster_count):
    sources, picks, count = lists.shape
    total = rows.shape[2] + FLAG_LANES
    return pl.pallas_call(
        functools.partial(dispatch_kernel, cluster_count),
        grid=(sources,),
        in_specs=[
            pl.BlockSpec(memory_space=pltpu.SMEM),
            pl.BlockSpec((sources, picks, count), lambda s: (0, 0, 0)),
            pl.BlockSpec((1, count, rows.shape[2]), lambda s: (s, 0, 0)),
        ],
        out_specs=pl.BlockSpec((owned, 1, cap, total), lambda s: (0, s, 0, 0)),
        out_shape=jax.ShapeDtypeStruct((owned, sources, cap, total), jnp.bfloat16),
        scratch_shapes=[
            pltpu.VMEM((sources, owned, count), jnp.int32),
            pltpu.VMEM((sources, FLAG_LANES, count), jnp.bfloat16),
        ],
        compiler_params=pltpu.CompilerParams(vmem_limit_bytes=48 * 2**20),
        cost_estimate=pl.CostEstimate(
            flops=2 * sources * owned * cap * count * total,
            bytes_accessed=2 * sources * (count * rows.shape[2] + owned * cap * total),
            transcendentals=0,
        ),
    )(first, lists, rows)


def block_kernel(base, near_count, scale, spots_ref, slots_ref, marks_ref, keep_ref, send_ref):
    mark_count = marks_ref.shape[1]
    depth = marks_ref.shape[2]
    parts, rows = keep_ref.shape[1], keep_ref.shape[2]
    cluster = base + pl.program_id(0)
    odd = spots_ref[spots_ref.shape[0] - 1] == 1
    factor = scale * math.log2(math.e)
    shift = LIFT * factor + 4.0 * math.log2(math.e)
    left = slots_ref[0, :, :depth]

    def kern(near_slot):
        marks = marks_ref[spots_ref[cluster * near_count + near_slot]]
        scores = lax.dot_general(
            left, marks, (((1,), (1,)), ((), ())), preferred_element_type=jnp.float32
        )
        return jnp.exp2(scores * factor - shift).astype(jnp.bfloat16)

    def store(block, column):
        width = block.shape[1]
        for part in range(parts):
            low = block[2 * part * rows : (2 * part + 1) * rows]
            high = block[(2 * part + 1) * rows : (2 * part + 2) * rows]
            keep_ref[0, part, :, column : column + width] = jnp.where(odd, high, low).astype(
                jnp.bfloat16
            )
            send_ref[0, part, :, column : column + width] = jnp.where(odd, low, high).astype(
                jnp.bfloat16
            )

    own = kern(0)
    turned = own.T
    for near_slot in range(near_count):
        other = own if near_slot == 0 else kern(near_slot)
        store(
            jnp.dot(turned, other, preferred_element_type=jnp.float32), near_slot * mark_count
        )
    store(
        jnp.dot(turned, slots_ref[0, :, depth:], preferred_element_type=jnp.float32),
        near_count * mark_count,
    )


def blocks(base, clusters, near_count, scale, parts, spots, slots, marks):
    mark_count, depth = marks.shape[1], marks.shape[2]
    slot_count = slots.shape[1]
    width = near_count * mark_count + slots.shape[2] - depth
    rows = mark_count // (2 * parts)
    shape = jax.ShapeDtypeStruct((clusters, parts, rows, width), jnp.bfloat16)
    spec = pl.BlockSpec((1, parts, rows, width), lambda a: (a, 0, 0, 0))
    return pl.pallas_call(
        functools.partial(block_kernel, base, near_count, scale),
        grid=(clusters,),
        in_specs=[
            pl.BlockSpec(memory_space=pltpu.SMEM),
            pl.BlockSpec((1, slot_count, slots.shape[2]), lambda a: (a + base, 0, 0)),
            pl.BlockSpec(marks.shape, lambda a: (0, 0, 0), pipeline_mode=pl.Buffered(1)),
        ],
        out_specs=[spec, spec],
        out_shape=[shape, shape],
        compiler_params=pltpu.CompilerParams(vmem_limit_bytes=48 * 2**20),
        cost_estimate=pl.CostEstimate(
            flops=2 * clusters * slot_count * width * (depth + mark_count),
            bytes_accessed=2 * marks.size + 2 * clusters * (slot_count * 768 + 256 * width),
            transcendentals=clusters * slot_count * width,
        ),
    )(spots, slots, marks)


def on_device(compounds, targets, cluster_lists, landmarks, neighbours):
    lmk_count = lax.axis_size("lmk")
    cmp_count = lax.axis_size("cmp")
    my_lmk = lax.axis_index("lmk")
    my_cmp = lax.axis_index("cmp")
    owned, mark_count, width = landmarks.shape
    rim = owned // 2
    near_count = neighbours.shape[1]
    cluster_count = neighbours.shape[0]
    cap = cluster_lists.shape[1] * (2 * compounds.shape[0] // cluster_count)
    scale = 0.75 * math.sqrt(width)
    first = my_lmk * owned

    rows = jnp.concatenate([normalize(compounds), targets], axis=1)
    all_rows = lax.all_gather(rows, "lmk")
    all_lists = lax.all_gather(cluster_lists.T, "lmk")

    forward = [(i, (i + 1) % lmk_count) for i in range(lmk_count)]
    backward = [(target, source) for source, target in forward]
    unit_marks = normalize(landmarks)
    low = lax.ppermute(unit_marks[owned - rim :], "lmk", forward)
    high = lax.ppermute(unit_marks[:rim], "lmk", backward)
    extended = jnp.concatenate([low, unit_marks, high], axis=0)
    lift = jnp.where(
        jnp.arange(owned + 2 * rim)[:, None, None] == jnp.arange(FLAG_LANES)[None, None, :],
        LIFT,
        0.0,
    ).astype(jnp.bfloat16)
    lift = jnp.broadcast_to(lift, (owned + 2 * rim, mark_count, FLAG_LANES))
    extended = jnp.concatenate([extended, lift], axis=2)

    near = lax.dynamic_slice_in_dim(neighbours, first, owned, 0)
    spots = jnp.mod(near - first + rim, cluster_count).reshape(-1)
    my_core = my_cmp % 2
    my_part = my_cmp // 2
    spots = jnp.concatenate([spots, my_core[None]]).astype(jnp.int32)

    slots = dispatch(
        jnp.asarray(first, jnp.int32)[None], all_lists, all_rows, owned, cap, cluster_count
    )
    slots = slots.reshape(owned, lmk_count * cap, slots.shape[3])
    parts = cmp_count // 2
    cores = [(i, i ^ 1) for i in range(cmp_count)]
    each = owned // CHUNKS
    done = []
    for chunk in range(CHUNKS):
        keep, send = blocks(
            chunk * each, each, near_count, scale, parts, spots, slots, extended
        )
        got = lax.ppermute(send, "cmp", cores)
        pieces = None
        for hop in range(parts - 1, -1, -1):
            part = (my_part + hop) % parts
            mine = lax.dynamic_index_in_dim(keep, part, 1, keepdims=False).astype(jnp.float32)
            mine += lax.dynamic_index_in_dim(got, part, 1, keepdims=False).astype(jnp.float32)
            if hop:
                across = [(i, (i + 2 * hop) % cmp_count) for i in range(cmp_count)]
                arrived = lax.ppermute(mine.astype(jnp.bfloat16), "cmp", across)
                arrived = arrived.astype(jnp.float32)
                pieces = arrived if pieces is None else pieces + arrived
            else:
                pieces = mine if pieces is None else pieces + mine
        done.append(jnp.transpose(pieces, (1, 0, 2)))
    shard = jnp.concatenate(done, axis=1)
    normal_blocks = shard[:, :, : near_count * mark_count].reshape(
        shard.shape[0], owned, near_count, mark_count
    )
    right_sides = shard[:, :, near_count * mark_count :]
    return (normal_blocks, right_sides)


def solution(mesh):
    placed = (
        P(("cmp", "lmk"), None),
        P(("cmp", "lmk"), None),
        P(("cmp", "lmk"), None),
        P("lmk", None, None),
        P(),
    )
    return jax.shard_map(
        on_device,
        mesh=mesh,
        in_specs=placed,
        out_specs=(P("cmp", "lmk", None, None), P("cmp", "lmk", None)),
        check_vma=False,
    )
```

time: 1160 us -> 462 us (0.40); the launches traced: 1150 us -> 461 us
  local copies, waits for them, and re-layouts: 516 us -> 17.9 us
  waiting for transfers between devices: 465 us -> 138 us
  blocking collectives: 0 us -> 131 us
  Pallas kernels: 0 us -> 119 us
  matrix products: 101 us -> 0 us
  starting transfers between devices: 23.3 us -> 11.5 us
    gather x16 -> x0, local copies, waits for them, and re-layouts: 334 us -> none  [the longest x13 299 us: pack_slots(): first_seen = jnp.searchsorted(ordered, ordered, side='left')]
    reduce_scatter x1 -> x0, waiting for transfers between devices: 289 us -> none  [on_device(): lax.psum_scatter(jnp.einsum('krm,krc->mkc', first_cols, tiles, preferred_...]
    all_gather x0 -> x1, blocking collectives: none -> 131 us  [on_device(): all_lists = lax.all_gather(cluster_lists.T, 'lmk')]
    pallas_call x0 -> x5, Pallas kernels: none -> 119 us  [the longest x4 96.2 us: blocks(): pl.pallas_call(functools.partial(block_kernel, base, near_count, scale),...]
    dot_general x9 -> x0, matrix products: 101 us -> none  [the longest x8 75.7 us: owner_tiles(): lax.dot_general(rows, marks, (((2,), (2,)), ((0,), (0,))), preferred_elem...]
    ppermute x2 -> x10, waiting for transfers between devices: 163 us -> 85.6 us  [the longest x4 85.6 us: on_device(): arrived = lax.ppermute(mine.astype(jnp.bfloat16), 'cmp', across)]
    scatter x4 -> x0, local copies, waits for them, and re-layouts: 63.4 us -> none  [the longest x1 23.6 us: pack_slots(): row_buffer = jnp.zeros((total_slots, unit_rows.shape[1]), jnp.bfloat16).a...]
    all_gather x0 -> x1, waiting for transfers between devices: none -> 52.2 us  [on_device(): all_rows = lax.all_gather(rows, 'lmk')]
  transfers between devices with their start and end apart: 6 -> 11, of which waited for: 3 -> 5; matrix products, arithmetic and copies ran while one was open for 9% -> 6% of each run, Pallas kernels for 0% -> 16%
where the time goes in v1:
time: 462 us; the launch traced here: 461 us
  waiting for transfers between devices  138 us (30%)
  blocking collectives  131 us (28%)
  Pallas kernels  119 us (26%)
  other arithmetic  30 us (6%)
  local copies, waits for them, and re-layouts  17.9 us (4%)
  between operations  14.3 us (3%)
  starting transfers between devices  11.5 us (2%)
    all_gather x1, blocking collectives, on_device(): all_lists = lax.all_gather(cluster_lists.T, 'lmk')  131 us
    pallas_call x4, Pallas kernels, blocks(): pl.pallas_call(functools.partial(block_kernel, base, near_count, scale),...  96.2 us
    ppermute x4, waiting for transfers between devices, on_device(): arrived = lax.ppermute(mine.astype(jnp.bfloat16), 'cmp', across)  85.6 us
    all_gather x1, waiting for transfers between devices, on_device(): all_rows = lax.all_gather(rows, 'lmk')  52.2 us
    pallas_call x1, Pallas kernels, dispatch(): pl.pallas_call(functools.partial(dispatch_kernel, cluster_count), grid=(s...  22.5 us
    unnamed x13, local copies, waits for them, and re-layouts  10.6 us
    concatenate x1, other arithmetic, on_device(): extended = jnp.concatenate([extended, lift], axis=2)  10.2 us
  transfers between devices with their start and end apart: 11, of which 5 were waited for; matrix products, arithmetic and copies ran while one was open for 6% of the time, Pallas kernels for 16%

profile of v1, /device:TPU:0, one launch (start us, length us, event | category | flops | bytes accessed | tf_op | source)
XLA Modules:
  0.0 461.4 jit_solution(5568708555039100305)
XLA Ops:
  11.5 3.2 fusion
  16.0 2.5 fusion.15
  19.2 3.0 collective-permute-start
  22.2 3.0 collective-permute-start.1
  25.5 131.2 %all-gather.2.lists_ref = s32[8,4,1024]{2,1,0:T(4,128)S(1)} all-gather(s32[1,4,1024]{2,1,0:T(4,128)S(1)} %bitcast.49), channel_id=2, replica_groups=mesh['cmp'=4,'lmk'=8] {'lmk'}, dimensions={0}, use_global_device_ids=true | all-gather | bytes 147456 | tf_op jit(solution)/shard_map/all_gather | solution.py:187
  157.0 10.2 %pad_maximum_fusion.marks_ref = bf16[32,256,640]{2,1,0:T(8,128)(2,1)} fusion(bf16[32,256,128]{2,1,0:T(8,128)(2,1)S(1)} %broadcast_in_dim.27, bf16[8,256,512]{2,1,0:T(8,128)(2,1)} %collective-permute-done.1, bf16[16,256,512]{2,1,0:T(8,128)(2,1)} %copy-done, bf16[8,256,512]{2,1,0:T(8,128)(2,1)S(1)} %collective-permute-done), kind=kLoop, calls=%fused_computation.2 | loop fusion | flops 41943040 | bytes 20971520 | tf_op jit(solution)/shard_map/concatenate | solution.py:201
  167.2 52.2 %all-gather.5.cloned.1.call-done = bf16[8192,640]{1,0:T(8,128)(2,1)} async-done(((bf16[1024,640]{1,0:T(8,128)(2,1)}), bf16[8192,640]{1,0:T(8,128)(2,1)}) %all-gather.5.cloned.1.call-update) | async-done | bytes 10485776 | tf_op jit(solution)/shard_map/all_gather | solution.py:186
  219.5 22.5 %shard_map.68 = bf16[16,8,64,768]{3,2,1,0:T(8,128)(2,1)} custom-call(s32[1]{0:T(128)} %bitcast.1.first_ref, s32[8,4,1024]{2,1,0:T(4,128)S(1)} %all-gather.2.lists_ref, bf16[8,1024,640]{2,1,0:T(8,128)(2,1)} %bitcast.50), custom_call_target="tpu_custom_call" | custom-call | flops 12884901888 | bytes 23068672 | tf_op jit(solution)/shard_map/pallas_call | solution.py:81
  241.9 24.0 %shard_map.69 = (bf16[4,2,64,2176]{3,2,1,0:T(8,128)(2,1)S(1)}, bf16[4,2,64,2176]{3,2,1,0:T(8,128)(2,1)S(1)}) custom-call(s32[129]{0:T(256)S(1)} %pad_add_fusion.spots_ref, bf16[16,512,768]{2,1,0:T(8,128)(2,1)} %bitcast.51, bf16[32,256,640]{2,1,0:T(8,128)(2,1)} %pad_maximum_fusion.marks_ref), custom_call_target="tpu_custom_call" | custom-call | flops 7985954816 | bytes 18087936 | tf_op jit(solution)/shard_map/pallas_call | solution.py:153
  266.0 1.6 copy.37
  267.6 24.0 %shard_map.70 = (bf16[4,2,64,2176]{3,2,1,0:T(8,128)(2,1)S(1)}, bf16[4,2,64,2176]{3,2,1,0:T(8,128)(2,1)S(1)}) custom-call(s32[129]{0:T(256)S(1)} %pad_add_fusion.spots_ref, bf16[16,512,768]{2,1,0:T(8,128)(2,1)} %bitcast.52, bf16[32,256,640]{2,1,0:T(8,128)(2,1)} %pad_maximum_fusion.marks_ref), custom_call_target="tpu_custom_call" | custom-call | flops 7985954816 | bytes 18087936 | tf_op jit(solution)/shard_map/pallas_call | solution.py:153
  293.7 24.0 %shard_map.71 = (bf16[4,2,64,2176]{3,2,1,0:T(8,128)(2,1)S(1)}, bf16[4,2,64,2176]{3,2,1,0:T(8,128)(2,1)S(1)}) custom-call(s32[129]{0:T(256)S(1)} %pad_add_fusion.spots_ref, bf16[16,512,768]{2,1,0:T(8,128)(2,1)} %bitcast.53, bf16[32,256,640]{2,1,0:T(8,128)(2,1)} %pad_maximum_fusion.marks_ref), custom_call_target="tpu_custom_call" | custom-call | flops 7985954816 | bytes 18087936 | tf_op jit(solution)/shard_map/pallas_call | solution.py:153
  318.0 24.1 %shard_map.72 = (bf16[4,2,64,2176]{3,2,1,0:T(8,128)(2,1)S(1)}, bf16[4,2,64,2176]{3,2,1,0:T(8,128)(2,1)S(1)}) custom-call(s32[129]{0:T(256)S(1)} %pad_add_fusion.spots_ref, bf16[16,512,768]{2,1,0:T(8,128)(2,1)} %bitcast.54, bf16[32,256,640]{2,1,0:T(8,128)(2,1)} %pad_maximum_fusion.marks_ref), custom_call_target="tpu_custom_call" | custom-call | flops 7985954816 | bytes 18087936 | tf_op jit(solution)/shard_map/pallas_call | solution.py:153
  344.1 1.6 collective-permute-start.3
  349.4 1.6 collective-permute-start.7
  351.8 19.8 %collective-permute-done.3 = bf16[4,64,2176]{2,1,0:T(8,128)(2,1)S(1)} collective-permute-done((bf16[4,64,2176]{2,1,0:T(8,128)(2,1)S(1)}, bf16[4,64,2176]{2,1,0:T(8,128)(2,1)S(1)}, u32[]{:S(2)}, u32[]{:S(2)}) %collective-permute-start.3) | collective-permute-done | bytes 1114144 | tf_op jit(solution)/shard_map/ppermute | solution.py:229
  371.6 1.6 fusion.5
  373.2 22.3 %collective-permute-done.5 = bf16[4,64,2176]{2,1,0:T(8,128)(2,1)S(1)} collective-permute-done((bf16[4,64,2176]{2,1,0:T(8,128)(2,1)S(1)}, bf16[4,64,2176]{2,1,0:T(8,128)(2,1)S(1)}, u32[]{:S(2)}, u32[]{:S(2)}) %collective-permute-start.5) | collective-permute-done | bytes 1114144 | tf_op jit(solution)/shard_map/ppermute | solution.py:229
  395.5 1.6 fusion.4
  397.1 22.3 %collective-permute-done.7 = bf16[4,64,2176]{2,1,0:T(8,128)(2,1)S(1)} collective-permute-done((bf16[4,64,2176]{2,1,0:T(8,128)(2,1)S(1)}, bf16[4,64,2176]{2,1,0:T(8,128)(2,1)S(1)}, u32[]{:S(2)}, u32[]{:S(2)}) %collective-permute-start.7) | collective-permute-done | bytes 1114144 | tf_op jit(solution)/shard_map/ppermute | solution.py:229
  419.4 1.6 fusion.3
  421.0 21.3 %collective-permute-done.9 = bf16[4,64,2176]{2,1,0:T(8,128)(2,1)S(1)} collective-permute-done((bf16[4,64,2176]{2,1,0:T(8,128)(2,1)S(1)}, bf16[4,64,2176]{2,1,0:T(8,128)(2,1)S(1)}, u32[]{:S(2)}, u32[]{:S(2)}) %collective-permute-start.9) | collective-permute-done | bytes 1114144 | tf_op jit(solution)/shard_map/ppermute | solution.py:229
  446.1 4.1 copy.50
  450.2 4.4 copy.47
  (47 shorter events, 19.4 us)
Async XLA Ops:
  7.2 3.1 copy-start.2
  7.2 212.3 %all-gather.5.cloned.1.call-start = ((), (), s32[]{:S(2)}) async-start(), calls=%async_computation | async-start | bytes 11796480 | tf_op jit(solution)/shard_map/all_gather | solution.py:186
  11.5 3.5 copy-start.1
  15.9 3.3 copy-start
  15.9 9.3 %copy-start.4 = (s32[128,8]{0,1:T(8,128)S(1)}, s32[128,8]{0,1:T(8,128)}, u32[]{:S(2)}) copy-start(s32[128,8]{0,1:T(8,128)} %param.9) | copy-start | bytes 12292
  16.0 9.5 %copy-start.3 = (s32[1024,4]{0,1:T(4,128)S(1)}, s32[1024,4]{0,1:T(4,128)}, u32[]{:S(2)}) copy-start(s32[1024,4]{0,1:T(4,128)} %param.7) | copy-start | bytes 49156
  19.2 137.5 %collective-permute-start = (bf16[8,256,512]{2,1,0:T(8,128)(2,1)}, bf16[8,256,512]{2,1,0:T(8,128)(2,1)S(1)}, u32[]{:S(2)}, u32[]{:S(2)}) collective-permute-start(bf16[8,256,512]{2,1,0:T(8,128)(2,1)} %get-tuple-element.24), channel_id=1, source_target_pairs={{0,1},{1,2},{2,3},{3,4},{4,5},{5,6},{6,7},{7,0},{8,9},{9,10},{10,1... | collective-permute-start | bytes 6291464 | tf_op jit(solution)/shard_map/ppermute | solution.py:192
  22.2 134.5 %collective-permute-start.1 = (bf16[8,256,512]{2,1,0:T(8,128)(2,1)}, bf16[8,256,512]{2,1,0:T(8,128)(2,1)}, u32[]{:S(2)}, u32[]{:S(2)}) collective-permute-start(bf16[8,256,512]{2,1,0:T(8,128)(2,1)} %get-tuple-element.25), channel_id=1, source_target_pairs={{1,0},{2,1},{3,2},{4,3},{5,4},{6,5},{7,6},{0,7},{9,8},{10,9},{11,1... | collective-permute-start | bytes 6291464 | tf_op jit(solution)/shard_map/ppermute | solution.py:193
  267.6 75.0 %collective-permute-start.2 = (bf16[4,2,64,2176]{3,2,0,1:T(8,128)(2,1)}, bf16[4,2,64,2176]{3,2,0,1:T(8,128)(2,1)}, u32[]{:S(2)}, u32[]{:S(2)}) collective-permute-start(bf16[4,2,64,2176]{3,2,0,1:T(8,128)(2,1)} %copy.37), channel_id=1, source_target_pairs={{0,8},{8,0},{16,24},{24,16},{1,9},{9,1},{17,25},{25,17},{2,10},{10... | collective-permute-start | bytes 6684680 | tf_op jit(solution)/shard_map/ppermute | solution.py:221
  293.2 52.5 %collective-permute-start.4 = (bf16[4,2,64,2176]{3,2,0,1:T(8,128)(2,1)}, bf16[4,2,64,2176]{3,2,0,1:T(8,128)(2,1)}, u32[]{:S(2)}, u32[]{:S(2)}) collective-permute-start(bf16[4,2,64,2176]{3,2,0,1:T(8,128)(2,1)} %copy.40), channel_id=1, source_target_pairs={{0,8},{8,0},{16,24},{24,16},{1,9},{9,1},{17,25},{25,17},{2,10},{10... | collective-permute-start | bytes 6684680 | tf_op jit(solution)/shard_map/ppermute | solution.py:221
  317.9 29.9 %collective-permute-start.6 = (bf16[4,2,64,2176]{3,2,0,1:T(8,128)(2,1)S(1)}, bf16[4,2,64,2176]{3,2,0,1:T(8,128)(2,1)}, u32[]{:S(2)}, u32[]{:S(2)}) collective-permute-start(bf16[4,2,64,2176]{3,2,0,1:T(8,128)(2,1)S(1)} %copy.43), channel_id=1, source_target_pairs={{0,8},{8,0},{16,24},{24,16},{1,9},{9,1},{17,25},{25,17},{2,10},{10... | collective-permute-start | bytes 6684680 | tf_op jit(solution)/shard_map/ppermute | solution.py:221
  342.0 8.9 %collective-permute-start.8 = (bf16[4,2,64,2176]{3,2,1,0:T(8,128)(2,1)S(1)}, bf16[4,2,64,2176]{3,2,1,0:T(8,128)(2,1)S(1)}, u32[]{:S(2)}, u32[]{:S(2)}) collective-permute-start(bf16[4,2,64,2176]{3,2,1,0:T(8,128)(2,1)S(1)} %get-tuple-element.17), channel_id=1, source_target_pairs={{0,8},{8,0},{16,24},{24,16},{1,9},{9,1},{17,25},{25,17},{2,10},{10... | collective-permute-start | bytes 6684680 | tf_op jit(solution)/shard_map/ppermute | solution.py:221
  344.1 27.5 %collective-permute-start.3 = (bf16[4,64,2176]{2,1,0:T(8,128)(2,1)S(1)}, bf16[4,64,2176]{2,1,0:T(8,128)(2,1)S(1)}, u32[]{:S(2)}, u32[]{:S(2)}) collective-permute-start(bf16[4,64,2176]{2,1,0:T(8,128)(2,1)S(1)} %fusion.8), channel_id=1, source_target_pairs={{0,16},{8,24},{16,0},{24,8},{1,17},{9,25},{17,1},{25,9},{2,18},{10... | collective-permute-start | bytes 3342344 | tf_op jit(solution)/shard_map/ppermute | solution.py:229
  347.2 48.3 %collective-permute-start.5 = (bf16[4,64,2176]{2,1,0:T(8,128)(2,1)S(1)}, bf16[4,64,2176]{2,1,0:T(8,128)(2,1)S(1)}, u32[]{:S(2)}, u32[]{:S(2)}) collective-permute-start(bf16[4,64,2176]{2,1,0:T(8,128)(2,1)S(1)} %fusion.9), channel_id=1, source_target_pairs={{0,16},{8,24},{16,0},{24,8},{1,17},{9,25},{17,1},{25,9},{2,18},{10... | collective-permute-start | bytes 3342344 | tf_op jit(solution)/shard_map/ppermute | solution.py:229
  349.4 70.0 %collective-permute-start.7 = (bf16[4,64,2176]{2,1,0:T(8,128)(2,1)S(1)}, bf16[4,64,2176]{2,1,0:T(8,128)(2,1)S(1)}, u32[]{:S(2)}, u32[]{:S(2)}) collective-permute-start(bf16[4,64,2176]{2,1,0:T(8,128)(2,1)S(1)} %fusion.10), channel_id=1, source_target_pairs={{0,16},{8,24},{16,0},{24,8},{1,17},{9,25},{17,1},{25,9},{2,18},{10... | collective-permute-start | bytes 3342344 | tf_op jit(solution)/shard_map/ppermute | solution.py:229
  351.2 91.1 %collective-permute-start.9 = (bf16[4,64,2176]{2,1,0:T(8,128)(2,1)S(1)}, bf16[4,64,2176]{2,1,0:T(8,128)(2,1)S(1)}, u32[]{:S(2)}, u32[]{:S(2)}) collective-permute-start(bf16[4,64,2176]{2,1,0:T(8,128)(2,1)S(1)} %fusion.11), channel_id=1, source_target_pairs={{0,16},{8,24},{16,0},{24,8},{1,17},{9,25},{17,1},{25,9},{2,18},{10... | collective-permute-start | bytes 3342344 | tf_op jit(solution)/shard_map/ppermute | solution.py:229
Sparse Core Ops, SparseCore 0:
  11.6 207.8 all-gather.4

commit v2 on v1

--- a/solution.py
+++ b/solution.py
@@ -183,8 +183,15 @@
     first = my_lmk * owned
 
     rows = jnp.concatenate([normalize(compounds), targets], axis=1)
-    all_rows = lax.all_gather(rows, "lmk")
-    all_lists = lax.all_gather(cluster_lists.T, "lmk")
+    count, lanes = rows.shape
+    picks = cluster_lists.shape[1]
+    per_pick = -(-count // lanes)
+    listed = jnp.pad(cluster_lists.T.astype(jnp.bfloat16), ((0, 0), (0, per_pick * lanes - count)))
+    listed = listed.reshape(picks * per_pick, lanes)
+    listed = jnp.pad(listed, ((0, -(picks * per_pick) % 16), (0, 0)))
+    all_rows = lax.all_gather(jnp.concatenate([rows, listed], axis=0), "lmk")
+    all_lists = all_rows[:, count : count + picks * per_pick].reshape(lmk_count, picks, -1)
+    all_lists = all_lists[:, :, :count].astype(jnp.int32)
 
     forward = [(i, (i + 1) % lmk_count) for i in range(lmk_count)]
     backward = [(target, source) for source, target in forward]
@@ -214,23 +221,26 @@
     cores = [(i, i ^ 1) for i in range(cmp_count)]
     each = owned // CHUNKS
     done = []
+    held = []
     for chunk in range(CHUNKS):
+        if chunk > 1:
+            spots, *held[chunk - 2] = lax.optimization_barrier((spots, *held[chunk - 2]))
         keep, send = blocks(
             chunk * each, each, near_count, scale, parts, spots, slots, extended
         )
         got = lax.ppermute(send, "cmp", cores)
-        pieces = None
-        for hop in range(parts - 1, -1, -1):
+        sums = []
+        for hop in range(parts):
             part = (my_part + hop) % parts
             mine = lax.dynamic_index_in_dim(keep, part, 1, keepdims=False).astype(jnp.float32)
             mine += lax.dynamic_index_in_dim(got, part, 1, keepdims=False).astype(jnp.float32)
-            if hop:
-                across = [(i, (i + 2 * hop) % cmp_count) for i in range(cmp_count)]
-                arrived = lax.ppermute(mine.astype(jnp.bfloat16), "cmp", across)
-                arrived = arrived.astype(jnp.float32)
-                pieces = arrived if pieces is None else pieces + arrived
-            else:
-                pieces = mine if pieces is None else pieces + mine
+            sums.append(mine.astype(jnp.bfloat16) if hop else mine)
+        held.append(sums)
+    for sums in held:
+        pieces = sums[0]
+        for hop in range(1, parts):
+            across = [(i, (i + 2 * hop) % cmp_count) for i in range(cmp_count)]
+            pieces += lax.ppermute(sums[hop], "cmp", across).astype(jnp.float32)
         done.append(jnp.transpose(pieces, (1, 0, 2)))
     shard = jnp.concatenate(done, axis=1)
     normal_blocks = shard[:, :, : near_count * mark_count].reshape(

time: 462 us -> 446 us (0.965)
  blocking collectives: 131 us -> 0 us
  waiting for transfers between devices: 138 us -> 250 us
    all_gather x1 -> x0, blocking collectives: 131 us -> none  [on_device(): all_lists = lax.all_gather(cluster_lists.T, 'lmk')]
    ppermute x1, waiting for transfers between devices: 0.01 us -> 104 us  [on_device(): low = lax.ppermute(unit_marks[owned - rim:], 'lmk', forward)]
    all_gather x1, waiting for transfers between devices: 52.2 us -> 76.6 us  [on_device(): all_rows = lax.all_gather(jnp.concatenate([rows, listed], axis=0), 'lmk')]
    ppermute x4, waiting for transfers between devices: 85.6 us -> 67.6 us  [on_device(): pieces += lax.ppermute(sums[hop], 'cmp', across).astype(jnp.float32)]
    unnamed x13 -> x15, local copies, waits for them, and re-layouts: 10.6 us -> 11 us
  transfers between devices with their start and end apart: 11 -> 11, of which waited for: 5 -> 7; matrix products, arithmetic and copies ran while one was open for 6% -> 7% of each run, Pallas kernels for 16% -> 16%
where the time goes in v2:
time: 446 us; the launch traced here: 445 us
  waiting for transfers between devices  250 us (56%)
  Pallas kernels  119 us (27%)
  other arithmetic  29.8 us (7%)
  local copies, waits for them, and re-layouts  20.8 us (5%)
  between operations  14.3 us (3%)
  starting transfers between devices  11.3 us (3%)
    ppermute x1, waiting for transfers between devices, on_device(): low = lax.ppermute(unit_marks[owned - rim:], 'lmk', forward)  104 us
    pallas_call x4, Pallas kernels, blocks(): pl.pallas_call(functools.partial(block_kernel, base, near_count, scale),...  96.2 us
    all_gather x1, waiting for transfers between devices, on_device(): all_rows = lax.all_gather(jnp.concatenate([rows, listed], axis=0), 'lmk')  76.6 us
    ppermute x4, waiting for transfers between devices, on_device(): pieces += lax.ppermute(sums[hop], 'cmp', across).astype(jnp.float32)  67.6 us
    pallas_call x1, Pallas kernels, dispatch(): pl.pallas_call(functools.partial(dispatch_kernel, cluster_count), grid=(s...  22.5 us
    unnamed x15, local copies, waits for them, and re-layouts  11 us
    concatenate x1, other arithmetic, on_device(): extended = jnp.concatenate([extended, lift], axis=2)  10.1 us
  transfers between devices with their start and end apart: 11, of which 7 were waited for; matrix products, arithmetic and copies ran while one was open for 7% of the time, Pallas kernels for 16%

profile of v2, /device:TPU:0, one launch (start us, length us, event | category | flops | bytes accessed | tf_op | source)
XLA Modules:
  0.0 445.2 jit_solution(10909283931421074166)
XLA Ops:
  11.6 3.2 fusion
  16.0 2.5 fusion.15
  19.3 3.0 collective-permute-start
  22.2 3.0 collective-permute-start.1
  25.6 103.8 %collective-permute-done = bf16[8,256,512]{2,1,0:T(8,128)(2,1)S(1)} collective-permute-done((bf16[8,256,512]{2,1,0:T(8,128)(2,1)}, bf16[8,256,512]{2,1,0:T(8,128)(2,1)S(1)}, u32[]{:S(2)}, u32[]{:S(2)}) %collective-permute-start) | collective-permute-done | bytes 2097184 | tf_op jit(solution)/shard_map/ppermute | solution.py:199
  129.3 2.3 collective-permute-done.1
  131.9 10.1 %pad_maximum_fusion.marks_ref = bf16[32,256,640]{2,1,0:T(8,128)(2,1)} fusion(bf16[32,256,128]{2,1,0:T(8,128)(2,1)S(1)} %broadcast_in_dim.27, bf16[8,256,512]{2,1,0:T(8,128)(2,1)} %collective-permute-done.1, bf16[16,256,512]{2,1,0:T(8,128)(2,1)} %copy-done.1, bf16[8,256,512]{2,1,0:T(8,128)(2,1)S(1)} %collective-permute-done), kind=kLoop, calls=%fused_computation.2 | loop fusion | flops 41943040 | bytes 20971520 | tf_op jit(solution)/shard_map/concatenate | solution.py:208
  142.1 76.6 %all-gather.3.cloned.1.call-done = bf16[8320,640]{1,0:T(8,128)(2,1)} async-done(((bf16[1040,640]{1,0:T(8,128)(2,1)}), bf16[8320,640]{1,0:T(8,128)(2,1)}) %all-gather.3.cloned.1.call-update) | async-done | bytes 10649616 | tf_op jit(solution)/shard_map/all_gather | solution.py:192
  219.6 22.5 %shard_map.68 = bf16[16,8,64,768]{3,2,1,0:T(8,128)(2,1)} custom-call(s32[1]{0:T(128)} %bitcast.1.first_ref, s32[8,4,1024]{2,1,0:T(4,128)S(1)} %slice_convert_fusion.lists_ref, bf16[8,1040,640]{2,1,0:T(8,128)(2,1)} %bitcast.45), custom_call_target="tpu_custom_call" | custom-call | flops 12884901888 | bytes 23068672 | tf_op jit(solution)/shard_map/pallas_call | solution.py:81
  242.1 24.0 %shard_map.69 = (bf16[4,2,64,2176]{3,2,1,0:T(8,128)(2,1)S(1)}, bf16[4,2,64,2176]{3,2,1,0:T(8,128)(2,1)S(1)}) custom-call(s32[129]{0:T(256)S(1)} %pad_add_fusion.spots_ref, bf16[16,512,768]{2,1,0:T(8,128)(2,1)} %bitcast.46, bf16[32,256,640]{2,1,0:T(8,128)(2,1)} %pad_maximum_fusion.marks_ref), custom_call_target="tpu_custom_call" | custom-call | flops 7985954816 | bytes 18087936 | tf_op jit(solution)/shard_map/pallas_call | solution.py:153
  266.2 1.7 copy.23
  268.2 24.0 %shard_map.70 = (bf16[4,2,64,2176]{3,2,1,0:T(8,128)(2,1)S(1)}, bf16[4,2,64,2176]{3,2,1,0:T(8,128)(2,1)S(1)}) custom-call(s32[129]{0:T(256)S(1)} %pad_add_fusion.spots_ref, bf16[16,512,768]{2,1,0:T(8,128)(2,1)} %bitcast.47, bf16[32,256,640]{2,1,0:T(8,128)(2,1)} %pad_maximum_fusion.marks_ref), custom_call_target="tpu_custom_call" | custom-call | flops 7985954816 | bytes 18087936 | tf_op jit(solution)/shard_map/pallas_call | solution.py:153
  294.3 3.7 fusion.8
  299.5 24.0 %shard_map.71 = (bf16[4,2,64,2176]{3,2,1,0:T(8,128)(2,1)S(1)}, bf16[4,2,64,2176]{3,2,1,0:T(8,128)(2,1)S(1)}) custom-call(s32[129]{0:T(256)S(1)} %pad_add_fusion.spots_ref, bf16[16,512,768]{2,1,0:T(8,128)(2,1)} %bitcast.48, bf16[32,256,640]{2,1,0:T(8,128)(2,1)} %pad_maximum_fusion.marks_ref), custom_call_target="tpu_custom_call" | custom-call | flops 7985954816 | bytes 18087936 | tf_op jit(solution)/shard_map/pallas_call | solution.py:153
  323.6 1.5 copy.29
  325.1 2.1 fusion.9
  327.2 24.1 %shard_map.72 = (bf16[4,2,64,2176]{3,2,1,0:T(8,128)(2,1)S(1)}, bf16[4,2,64,2176]{3,2,1,0:T(8,128)(2,1)S(1)}) custom-call(s32[129]{0:T(256)S(1)} %pad_add_fusion.spots_ref, bf16[16,512,768]{2,1,0:T(8,128)(2,1)} %bitcast.49, bf16[32,256,640]{2,1,0:T(8,128)(2,1)} %pad_maximum_fusion.marks_ref), custom_call_target="tpu_custom_call" | custom-call | flops 7985954816 | bytes 18087936 | tf_op jit(solution)/shard_map/pallas_call | solution.py:153
  354.1 1.6 collective-permute-start.7
  356.7 22.5 %collective-permute-done.5 = bf16[4,64,2176]{2,1,0:T(8,128)(2,1)S(1)} collective-permute-done((bf16[4,64,2176]{2,1,0:T(8,128)(2,1)S(1)}, bf16[4,64,2176]{2,1,0:T(8,128)(2,1)S(1)}, u32[]{:S(2)}, u32[]{:S(2)}) %collective-permute-start.5) | collective-permute-done | bytes 1114144 | tf_op jit(solution)/shard_map/ppermute | solution.py:243
  379.5 23.7 %collective-permute-done.7 = bf16[4,64,2176]{2,1,0:T(8,128)(2,1)S(1)} collective-permute-done((bf16[4,64,2176]{2,1,0:T(8,128)(2,1)S(1)}, bf16[4,64,2176]{2,1,0:T(8,128)(2,1)S(1)}, u32[]{:S(2)}, u32[]{:S(2)}) %collective-permute-start.7) | collective-permute-done | bytes 1114144 | tf_op jit(solution)/shard_map/ppermute | solution.py:243
  403.2 1.6 fusion.4
  404.8 21.4 %collective-permute-done.9 = bf16[4,64,2176]{2,1,0:T(8,128)(2,1)S(1)} collective-permute-done((bf16[4,64,2176]{2,1,0:T(8,128)(2,1)S(1)}, bf16[4,64,2176]{2,1,0:T(8,128)(2,1)S(1)}, u32[]{:S(2)}, u32[]{:S(2)}) %collective-permute-start.9) | collective-permute-done | bytes 1114144 | tf_op jit(solution)/shard_map/ppermute | solution.py:243
  429.8 4.1 copy.36
  434.0 4.4 copy.33
  (54 shorter events, 19.4 us)
Async XLA Ops:
  7.2 3.1 copy-start.4
  7.2 3.2 copy-start.3
  7.2 211.4 %all-gather.3.cloned.1.call-start = ((), (), s32[]{:S(2)}) async-start(), calls=%async_computation | async-start | bytes 11980800 | tf_op jit(solution)/shard_map/all_gather | solution.py:192
  11.6 3.5 copy-start.2
  16.0 3.3 copy-start.1
  16.0 9.3 %copy-start.5 = (s32[128,8]{0,1:T(8,128)S(1)}, s32[128,8]{0,1:T(8,128)}, u32[]{:S(2)}) copy-start(s32[128,8]{0,1:T(8,128)} %param.9) | copy-start | bytes 12292
  19.3 110.1 %collective-permute-start = (bf16[8,256,512]{2,1,0:T(8,128)(2,1)}, bf16[8,256,512]{2,1,0:T(8,128)(2,1)S(1)}, u32[]{:S(2)}, u32[]{:S(2)}) collective-permute-start(bf16[8,256,512]{2,1,0:T(8,128)(2,1)} %get-tuple-element.38), channel_id=1, source_target_pairs={{0,1},{1,2},{2,3},{3,4},{4,5},{5,6},{6,7},{7,0},{8,9},{9,10},{10,1... | collective-permute-start | bytes 6291464 | tf_op jit(solution)/shard_map/ppermute | solution.py:199
  22.2 109.4 %collective-permute-start.1 = (bf16[8,256,512]{2,1,0:T(8,128)(2,1)}, bf16[8,256,512]{2,1,0:T(8,128)(2,1)}, u32[]{:S(2)}, u32[]{:S(2)}) collective-permute-start(bf16[8,256,512]{2,1,0:T(8,128)(2,1)} %get-tuple-element.39), channel_id=1, source_target_pairs={{1,0},{2,1},{3,2},{4,3},{5,4},{6,5},{7,6},{0,7},{9,8},{10,9},{11,1... | collective-permute-start | bytes 6291464 | tf_op jit(solution)/shard_map/ppermute | solution.py:200
  266.2 2.1 copy-start
  268.2 26.1 %collective-permute-start.2 = (bf16[4,2,64,2176]{3,2,0,1:T(8,128)(2,1)}, bf16[4,2,64,2176]{3,2,0,1:T(8,128)(2,1)}, u32[]{:S(2)}, u32[]{:S(2)}) collective-permute-start(bf16[4,2,64,2176]{3,2,0,1:T(8,128)(2,1)} %copy.23), channel_id=1, source_target_pairs={{0,8},{8,0},{16,24},{24,16},{1,9},{9,1},{17,25},{25,17},{2,10},{10... | collective-permute-start | bytes 6684680 | tf_op jit(solution)/shard_map/ppermute | solution.py:231
  293.8 31.3 %collective-permute-start.4 = (bf16[4,2,64,2176]{3,2,0,1:T(8,128)(2,1)}, bf16[4,2,64,2176]{3,2,0,1:T(8,128)(2,1)}, u32[]{:S(2)}, u32[]{:S(2)}) collective-permute-start(bf16[4,2,64,2176]{3,2,0,1:T(8,128)(2,1)} %copy.26), channel_id=1, source_target_pairs={{0,8},{8,0},{16,24},{24,16},{1,9},{9,1},{17,25},{25,17},{2,10},{10... | collective-permute-start | bytes 6684680 | tf_op jit(solution)/shard_map/ppermute | solution.py:231
  298.0 54.3 %collective-permute-start.3 = (bf16[4,64,2176]{2,1,0:T(8,128)(2,1)}, bf16[4,64,2176]{2,1,0:T(8,128)(2,1)S(1)}, u32[]{:S(2)}, u32[]{:S(2)}) collective-permute-start(bf16[4,64,2176]{2,1,0:T(8,128)(2,1)} %get-tuple-element.19), channel_id=1, source_target_pairs={{0,16},{8,24},{16,0},{24,8},{1,17},{9,25},{17,1},{25,9},{2,18},{10... | collective-permute-start | bytes 3342344 | tf_op jit(solution)/shard_map/ppermute | solution.py:243
  325.1 27.5 %collective-permute-start.6 = (bf16[4,2,64,2176]{3,2,0,1:T(8,128)(2,1)}, bf16[4,2,64,2176]{3,2,0,1:T(8,128)(2,1)}, u32[]{:S(2)}, u32[]{:S(2)}) collective-permute-start(bf16[4,2,64,2176]{3,2,0,1:T(8,128)(2,1)} %copy.29), channel_id=1, source_target_pairs={{0,8},{8,0},{16,24},{24,16},{1,9},{9,1},{17,25},{25,17},{2,10},{10... | collective-permute-start | bytes 6684680 | tf_op jit(solution)/shard_map/ppermute | solution.py:231
  351.3 4.5 %collective-permute-start.8 = (bf16[4,2,64,2176]{3,2,1,0:T(8,128)(2,1)S(1)}, bf16[4,2,64,2176]{3,2,1,0:T(8,128)(2,1)S(1)}, u32[]{:S(2)}, u32[]{:S(2)}) collective-permute-start(bf16[4,2,64,2176]{3,2,1,0:T(8,128)(2,1)S(1)} %get-tuple-element.29), channel_id=1, source_target_pairs={{0,8},{8,0},{16,24},{24,16},{1,9},{9,1},{17,25},{25,17},{2,10},{10... | collective-permute-start | bytes 6684680 | tf_op jit(solution)/shard_map/ppermute | solution.py:231
  351.9 27.4 %collective-permute-start.5 = (bf16[4,64,2176]{2,1,0:T(8,128)(2,1)S(1)}, bf16[4,64,2176]{2,1,0:T(8,128)(2,1)S(1)}, u32[]{:S(2)}, u32[]{:S(2)}) collective-permute-start(bf16[4,64,2176]{2,1,0:T(8,128)(2,1)S(1)} %get-tuple-element.24), channel_id=1, source_target_pairs={{0,16},{8,24},{16,0},{24,8},{1,17},{9,25},{17,1},{25,9},{2,18},{10... | collective-permute-start | bytes 3342344 | tf_op jit(solution)/shard_map/ppermute | solution.py:243
  354.1 49.0 %collective-permute-start.7 = (bf16[4,64,2176]{2,1,0:T(8,128)(2,1)S(1)}, bf16[4,64,2176]{2,1,0:T(8,128)(2,1)S(1)}, u32[]{:S(2)}, u32[]{:S(2)}) collective-permute-start(bf16[4,64,2176]{2,1,0:T(8,128)(2,1)S(1)} %fusion.10), channel_id=1, source_target_pairs={{0,16},{8,24},{16,0},{24,8},{1,17},{9,25},{17,1},{25,9},{2,18},{10... | collective-permute-start | bytes 3342344 | tf_op jit(solution)/shard_map/ppermute | solution.py:243
  356.1 70.0 %collective-permute-start.9 = (bf16[4,64,2176]{2,1,0:T(8,128)(2,1)S(1)}, bf16[4,64,2176]{2,1,0:T(8,128)(2,1)S(1)}, u32[]{:S(2)}, u32[]{:S(2)}) collective-permute-start(bf16[4,64,2176]{2,1,0:T(8,128)(2,1)S(1)} %fusion.11), channel_id=1, source_target_pairs={{0,16},{8,24},{16,0},{24,8},{1,17},{9,25},{17,1},{25,9},{2,18},{10... | collective-permute-start | bytes 3342344 | tf_op jit(solution)/shard_map/ppermute | solution.py:243
Sparse Core Ops, SparseCore 0:
  11.7 206.8 all-gather.2

commit v3 on v2

--- a/solution.py
+++ b/solution.py
@@ -10,7 +10,7 @@
 
 LIFT = 8.0
 FLAG_LANES = 128
-CHUNKS = 4
+CHUNKS = 8
 
 
 def normalize(data):
@@ -162,9 +162,9 @@
         out_shape=[shape, shape],
         compiler_params=pltpu.CompilerParams(vmem_limit_bytes=48 * 2**20),
         cost_estimate=pl.CostEstimate(
-            flops=2 * clusters * slot_count * width * (depth + mark_count),
-            bytes_accessed=2 * marks.size + 2 * clusters * (slot_count * 768 + 256 * width),
-            transcendentals=clusters * slot_count * width,
+            flops=2**20,
+            bytes_accessed=2**20,
+            transcendentals=0,
         ),
     )(spots, slots, marks)
 
@@ -196,9 +196,20 @@
     forward = [(i, (i + 1) % lmk_count) for i in range(lmk_count)]
     backward = [(target, source) for source, target in forward]
     unit_marks = normalize(landmarks)
-    low = lax.ppermute(unit_marks[owned - rim :], "lmk", forward)
-    high = lax.ppermute(unit_marks[:rim], "lmk", backward)
-    extended = jnp.concatenate([low, unit_marks, high], axis=0)
+    portion = mark_count // cmp_count
+    quarter = lax.dynamic_slice_in_dim(unit_marks, my_cmp * portion, portion, 1)
+    low = lax.ppermute(quarter[owned - rim :], "lmk", forward)
+    high = lax.ppermute(quarter[:rim], "lmk", backward)
+    rims = jnp.concatenate([low, high], axis=0)
+    edges = jnp.zeros((2 * rim, cmp_count, portion, width), jnp.bfloat16)
+    for turn in range(cmp_count):
+        swap = [(i, i ^ turn) for i in range(cmp_count)]
+        piece = lax.ppermute(rims, "cmp", swap) if turn else rims
+        edges = lax.dynamic_update_slice_in_dim(
+            edges, piece[:, None], jnp.bitwise_xor(my_cmp, turn), 1
+        )
+    edges = edges.reshape(2 * rim, mark_count, width)
+    extended = jnp.concatenate([edges[:rim], unit_marks, edges[rim:]], axis=0)
     lift = jnp.where(
         jnp.arange(owned + 2 * rim)[:, None, None] == jnp.arange(FLAG_LANES)[None, None, :],
         LIFT,
@@ -222,9 +233,21 @@
     each = owned // CHUNKS
     done = []
     held = []
+    crossed = []
+
+    def cross(sums):
+        pieces = []
+        for hop in range(1, parts):
+            across = [(i, (i + 2 * hop) % cmp_count) for i in range(cmp_count)]
+            pieces.append(lax.ppermute(sums[hop], "cmp", across))
+        return pieces
+
     for chunk in range(CHUNKS):
         if chunk > 1:
             spots, *held[chunk - 2] = lax.optimization_barrier((spots, *held[chunk - 2]))
+            crossed.append(cross(held[chunk - 2]))
+        if chunk > 2:
+            spots, *crossed[chunk - 3] = lax.optimization_barrier((spots, *crossed[chunk - 3]))
         keep, send = blocks(
             chunk * each, each, near_count, scale, parts, spots, slots, extended
         )
@@ -236,11 +259,11 @@
             mine += lax.dynamic_index_in_dim(got, part, 1, keepdims=False).astype(jnp.float32)
             sums.append(mine.astype(jnp.bfloat16) if hop else mine)
         held.append(sums)
-    for sums in held:
+    crossed += [cross(sums) for sums in held[len(crossed) :]]
+    for sums, arrived in zip(held, crossed):
         pieces = sums[0]
-        for hop in range(1, parts):
-            across = [(i, (i + 2 * hop) % cmp_count) for i in range(cmp_count)]
-            pieces += lax.ppermute(sums[hop], "cmp", across).astype(jnp.float32)
+        for piece in arrived:
+            pieces += piece.astype(jnp.float32)
         done.append(jnp.transpose(pieces, (1, 0, 2)))
     shard = jnp.concatenate(done, axis=1)
     normal_blocks = shard[:, :, : near_count * mark_count].reshape(

time: 446 us -> 398 us (0.89)
  waiting for transfers between devices: 250 us -> 166 us
  Pallas kernels: 119 us -> 137 us
  starting transfers between devices: 11.3 us -> 18.3 us
    ppermute x6 -> x13, waiting for transfers between devices: 174 us -> 101 us  [the longest x3 44.5 us: on_device(): piece = lax.ppermute(rims, 'cmp', swap) if turn else rims]
    pallas_call x4 -> x8, Pallas kernels: 96.2 us -> 114 us  [blocks(): pl.pallas_call(functools.partial(block_kernel, base, near_count, scale),...]
    all_gather x1, waiting for transfers between devices: 76.6 us -> 62.2 us  [on_device(): all_rows = lax.all_gather(jnp.concatenate([rows, listed], axis=0), 'lmk')]
    ppermute x6 -> x13, starting transfers between devices: 10.2 us -> 16.9 us  [the longest x8 8.75 us: cross(): pieces.append(lax.ppermute(sums[hop], 'cmp', across))]
    convert_element_type x4 -> x7, other arithmetic: 7.65 us -> 12.5 us  [on_device(): sums.append(mine.astype(jnp.bfloat16) if hop else mine)]
    unnamed x15 -> x18, local copies, waits for them, and re-layouts: 11 us -> 14.2 us
  transfers between devices with their start and end apart: 11 -> 22, of which waited for: 7 -> 9; matrix products, arithmetic and copies ran while one was open for 7% -> 9% of each run, Pallas kernels for 16% -> 22%
where the time goes in v3:
time: 398 us; the launch traced here: 393 us
  waiting for transfers between devices  166 us (42%)
  Pallas kernels  137 us (34%)
  other arithmetic  33.4 us (8%)
  local copies, waits for them, and re-layouts  23.9 us (6%)
  starting transfers between devices  18.3 us (5%)
  between operations  14.8 us (4%)
    pallas_call x8, Pallas kernels, blocks(): pl.pallas_call(functools.partial(block_kernel, base, near_count, scale),...  114 us
    all_gather x1, waiting for transfers between devices, on_device(): all_rows = lax.all_gather(jnp.concatenate([rows, listed], axis=0), 'lmk')  62.2 us
    ppermute x3, waiting for transfers between devices, on_device(): piece = lax.ppermute(rims, 'cmp', swap) if turn else rims  44.5 us
    ppermute x1, waiting for transfers between devices, on_device(): low = lax.ppermute(quarter[owned - rim:], 'lmk', forward)  28.5 us
    ppermute x8, waiting for transfers between devices, cross(): pieces.append(lax.ppermute(sums[hop], 'cmp', across))  23.8 us
    pallas_call x1, Pallas kernels, dispatch(): pl.pallas_call(functools.partial(dispatch_kernel, cluster_count), grid=(s...  22.6 us
    unnamed x18, local copies, waits for them, and re-layouts  14.2 us
    convert_element_type x7, other arithmetic, on_device(): sums.append(mine.astype(jnp.bfloat16) if hop else mine)  12.5 us
  transfers between devices with their start and end apart: 22, of which 9 were waited for; matrix products, arithmetic and copies ran while one was open for 9% of the time, Pallas kernels for 22%

profile of v3, /device:TPU:0, one launch (start us, length us, event | category | flops | bytes accessed | tf_op | source)
XLA Modules:
  0.0 393.2 jit_solution(2457342061218878539)
XLA Ops:
  11.2 3.2 fusion
  17.7 3.0 collective-permute-start
  20.7 3.1 collective-permute-start.1
  23.8 28.5 %collective-permute-done = bf16[8,64,512]{2,1,0:T(8,128)(2,1)S(1)} collective-permute-done((bf16[8,64,512]{2,1,0:T(8,128)(2,1)S(1)}, bf16[8,64,512]{2,1,0:T(8,128)(2,1)S(1)}, u32[]{:S(2)}, u32[]{:S(2)}) %collective-permute-start) | collective-permute-done | bytes 524320 | tf_op jit(solution)/shard_map/ppermute | solution.py:201
  52.4 4.0 %collective-permute-done.1 = bf16[8,64,512]{2,1,0:T(8,128)(2,1)S(1)} collective-permute-done((bf16[8,64,512]{2,1,0:T(8,128)(2,1)S(1)}, bf16[8,64,512]{2,1,0:T(8,128)(2,1)S(1)}, u32[]{:S(2)}, u32[]{:S(2)}) %collective-permute-start.1) | collective-permute-done | bytes 524320 | tf_op jit(solution)/shard_map/ppermute | solution.py:202
  59.5 23.1 %collective-permute-done.3 = bf16[16,64,512]{2,1,0:T(8,128)(2,1)S(1)} collective-permute-done((bf16[16,64,512]{2,1,0:T(8,128)(2,1)S(1)}, bf16[16,64,512]{2,1,0:T(8,128)(2,1)S(1)}, u32[]{:S(2)}, u32[]{:S(2)}) %collective-permute-start.3) | collective-permute-done | bytes 1048608 | tf_op jit(solution)/shard_map/ppermute | solution.py:207
  82.6 21.5 %collective-permute-done.4 = bf16[16,64,512]{2,1,0:T(8,128)(2,1)S(1)} collective-permute-done((bf16[16,64,512]{2,1,0:T(8,128)(2,1)S(1)}, bf16[16,64,512]{2,1,0:T(8,128)(2,1)S(1)}, u32[]{:S(2)}, u32[]{:S(2)}) %collective-permute-start.4) | collective-permute-done | bytes 1048608 | tf_op jit(solution)/shard_map/ppermute | solution.py:207
  106.4 8.6 %pad_maximum_fusion.marks_ref = bf16[32,256,640]{2,1,0:T(8,128)(2,1)} fusion(bf16[32,256,128]{2,1,0:T(8,128)(2,1)S(1)} %broadcast_in_dim.47, bf16[8,256,512]{2,1,0:T(8,128)(2,1)S(1)} %bitcast.95, bf16[16,256,512]{2,1,0:T(8,128)(2,1)S(1)} %copy-done.1, bf16[8,256,512]{2,1,0:T(8,128)(2,1)S(1)} %bitcast.94), kind=kLoop, calls=%fused_computation.2 | loop fusion | flops 41943040 | bytes 20971520 | tf_op jit(solution)/shard_map/concatenate | solution.py:219
  115.0 62.2 %all-gather.3.cloned.1.call-done = bf16[8320,640]{1,0:T(8,128)(2,1)} async-done(((bf16[1040,640]{1,0:T(8,128)(2,1)}), bf16[8320,640]{1,0:T(8,128)(2,1)}) %all-gather.3.cloned.1.call-update) | async-done | bytes 10649616 | tf_op jit(solution)/shard_map/all_gather | solution.py:192
  178.2 22.6 %shard_map.68 = bf16[16,8,64,768]{3,2,1,0:T(8,128)(2,1)} custom-call(s32[1]{0:T(128)} %bitcast.1.first_ref, s32[8,4,1024]{2,1,0:T(4,128)S(1)} %slice_convert_fusion.lists_ref, bf16[8,1040,640]{2,1,0:T(8,128)(2,1)} %bitcast.97), custom_call_target="tpu_custom_call" | custom-call | flops 12884901888 | bytes 23068672 | tf_op jit(solution)/shard_map/pallas_call | solution.py:81
  200.8 14.2 %shard_map.70 = (bf16[2,2,64,2176]{3,2,1,0:T(8,128)(2,1)S(1)}, bf16[2,2,64,2176]{3,2,1,0:T(8,128)(2,1)S(1)}) custom-call(s32[129]{0:T(256)S(1)} %pad_add_fusion.spots_ref, bf16[16,512,768]{2,1,0:T(8,128)(2,1)} %bitcast.84, bf16[32,256,640]{2,1,0:T(8,128)(2,1)} %pad_maximum_fusion.marks_ref), custom_call_target="tpu_custom_call" | custom-call | flops 1048576 | bytes 1048576 | tf_op jit(solution)/shard_map/pallas_call | solution.py:153
  215.0 14.2 %shard_map.69 = (bf16[2,2,64,2176]{3,2,1,0:T(8,128)(2,1)S(1)}, bf16[2,2,64,2176]{3,2,1,0:T(8,128)(2,1)S(1)}) custom-call(s32[129]{0:T(256)S(1)} %pad_add_fusion.spots_ref, bf16[16,512,768]{2,1,0:T(8,128)(2,1)} %bitcast.85, bf16[32,256,640]{2,1,0:T(8,128)(2,1)} %pad_maximum_fusion.marks_ref), custom_call_target="tpu_custom_call" | custom-call | flops 1048576 | bytes 1048576 | tf_op jit(solution)/shard_map/pallas_call | solution.py:153
  234.1 3.4 fusion.6
  239.0 14.3 %shard_map.71 = (bf16[2,2,64,2176]{3,2,1,0:T(8,128)(2,1)S(1)}, bf16[2,2,64,2176]{3,2,1,0:T(8,128)(2,1)S(1)}) custom-call(s32[129]{0:T(256)S(1)} %pad_add_fusion.spots_ref, bf16[16,512,768]{2,1,0:T(8,128)(2,1)} %bitcast.86, bf16[32,256,640]{2,1,0:T(8,128)(2,1)} %pad_maximum_fusion.marks_ref), custom_call_target="tpu_custom_call" | custom-call | flops 1048576 | bytes 1048576 | tf_op jit(solution)/shard_map/pallas_call | solution.py:153
  255.0 14.2 %shard_map.72 = (bf16[2,2,64,2176]{3,2,1,0:T(8,128)(2,1)S(1)}, bf16[2,2,64,2176]{3,2,1,0:T(8,128)(2,1)S(1)}) custom-call(s32[129]{0:T(256)S(1)} %pad_add_fusion.spots_ref, bf16[16,512,768]{2,1,0:T(8,128)(2,1)} %bitcast.87, bf16[32,256,640]{2,1,0:T(8,128)(2,1)} %pad_maximum_fusion.marks_ref), custom_call_target="tpu_custom_call" | custom-call | flops 1048576 | bytes 1048576 | tf_op jit(solution)/shard_map/pallas_call | solution.py:153
  271.6 2.4 fusion.8
  275.5 14.2 %shard_map.73 = (bf16[2,2,64,2176]{3,2,1,0:T(8,128)(2,1)S(1)}, bf16[2,2,64,2176]{3,2,1,0:T(8,128)(2,1)S(1)}) custom-call(s32[129]{0:T(256)S(1)} %pad_add_fusion.spots_ref, bf16[16,512,768]{2,1,0:T(8,128)(2,1)} %bitcast.88, bf16[32,256,640]{2,1,0:T(8,128)(2,1)} %pad_maximum_fusion.marks_ref), custom_call_target="tpu_custom_call" | custom-call | flops 1048576 | bytes 1048576 | tf_op jit(solution)/shard_map/pallas_call | solution.py:153
  293.1 14.4 %shard_map.74 = (bf16[2,2,64,2176]{3,2,1,0:T(8,128)(2,1)S(1)}, bf16[2,2,64,2176]{3,2,1,0:T(8,128)(2,1)S(1)}) custom-call(s32[129]{0:T(256)S(1)} %pad_add_fusion.spots_ref, bf16[16,512,768]{2,1,0:T(8,128)(2,1)} %bitcast.89, bf16[32,256,640]{2,1,0:T(8,128)(2,1)} %pad_maximum_fusion.marks_ref), custom_call_target="tpu_custom_call" | custom-call | flops 1048576 | bytes 1048576 | tf_op jit(solution)/shard_map/pallas_call | solution.py:153
  313.9 14.2 %shard_map.75 = (bf16[2,2,64,2176]{3,2,1,0:T(8,128)(2,1)S(1)}, bf16[2,2,64,2176]{3,2,1,0:T(8,128)(2,1)S(1)}) custom-call(s32[129]{0:T(256)S(1)} %pad_add_fusion.spots_ref, bf16[16,512,768]{2,1,0:T(8,128)(2,1)} %bitcast.90, bf16[32,256,640]{2,1,0:T(8,128)(2,1)} %pad_maximum_fusion.marks_ref), custom_call_target="tpu_custom_call" | custom-call | flops 1048576 | bytes 1048576 | tf_op jit(solution)/shard_map/pallas_call | solution.py:153
  332.2 14.4 %shard_map.76 = (bf16[2,2,64,2176]{3,2,1,0:T(8,128)(2,1)S(1)}, bf16[2,2,64,2176]{3,2,1,0:T(8,128)(2,1)S(1)}) custom-call(s32[129]{0:T(256)S(1)} %pad_add_fusion.spots_ref, bf16[16,512,768]{2,1,0:T(8,128)(2,1)} %bitcast.91, bf16[32,256,640]{2,1,0:T(8,128)(2,1)} %pad_maximum_fusion.marks_ref), custom_call_target="tpu_custom_call" | custom-call | flops 1048576 | bytes 1048576 | tf_op jit(solution)/shard_map/pallas_call | solution.py:153
  351.1 12.6 %collective-permute-done.18 = bf16[2,64,2176]{2,1,0:T(8,128)(2,1)S(1)} collective-permute-done((bf16[2,64,2176]{2,1,0:T(8,128)(2,1)S(1)}, bf16[2,64,2176]{2,1,0:T(8,128)(2,1)S(1)}, u32[]{:S(2)}, u32[]{:S(2)}) %collective-permute-start.18) | collective-permute-done | bytes 557088 | tf_op jit(solution)/shard_map/ppermute | solution.py:242
  364.0 11.1 %collective-permute-done.20 = bf16[2,64,2176]{2,1,0:T(8,128)(2,1)S(1)} collective-permute-done((bf16[2,64,2176]{2,1,0:T(8,128)(2,1)S(1)}, bf16[2,64,2176]{2,1,0:T(8,128)(2,1)S(1)}, u32[]{:S(2)}, u32[]{:S(2)}) %collective-permute-start.20) | collective-permute-done | bytes 557088 | tf_op jit(solution)/shard_map/ppermute | solution.py:242
  376.5 4.1 %copy.68 = f32[128,8,8,256]{3,2,1,0:T(8,128)S(1)} copy(f32[128,8,8,256]{3,1,2,0:T(8,128)S(1)} %bitcast.92) | data formatting | bytes 16777216
  380.6 4.4 %copy.65 = f32[64,16,8,256]{3,2,1,0:T(8,128)} copy(f32[64,16,8,256]{3,2,0,1:T(8,128)S(1)} %bitcast.93) | data formatting | bytes 16777216
  (100 shorter events, 46.4 us)
Async XLA Ops:
  7.2 170.0 %all-gather.3.cloned.1.call-start = ((), (), s32[]{:S(2)}) async-start(), calls=%async_computation | async-start | bytes 11980800 | tf_op jit(solution)/shard_map/all_gather | solution.py:192
  11.2 3.5 copy-start.2
  17.7 40.4 %copy-start.6 = (s32[128,8]{0,1:T(8,128)S(1)}, s32[128,8]{0,1:T(8,128)}, u32[]{:S(2)}) copy-start(s32[128,8]{0,1:T(8,128)} %param.9) | copy-start | bytes 12292
  17.7 34.7 %collective-permute-start = (bf16[8,64,512]{2,1,0:T(8,128)(2,1)S(1)}, bf16[8,64,512]{2,1,0:T(8,128)(2,1)S(1)}, u32[]{:S(2)}, u32[]{:S(2)}) collective-permute-start(bf16[8,64,512]{2,1,0:T(8,128)(2,1)S(1)} %get-tuple-element.97), channel_id=1, source_target_pairs={{0,1},{1,2},{2,3},{3,4},{4,5},{5,6},{6,7},{7,0},{8,9},{9,10},{10,1... | collective-permute-start | bytes 1572872 | tf_op jit(solution)/shard_map/ppermute | solution.py:201
  20.7 35.7 %collective-permute-start.1 = (bf16[8,64,512]{2,1,0:T(8,128)(2,1)S(1)}, bf16[8,64,512]{2,1,0:T(8,128)(2,1)S(1)}, u32[]{:S(2)}, u32[]{:S(2)}) collective-permute-start(bf16[8,64,512]{2,1,0:T(8,128)(2,1)S(1)} %get-tuple-element.96), channel_id=1, source_target_pairs={{1,0},{2,1},{3,2},{4,3},{5,4},{6,5},{7,6},{0,7},{9,8},{10,9},{11,1... | collective-permute-start | bytes 1572872 | tf_op jit(solution)/shard_map/ppermute | solution.py:202
  56.4 2.9 collective-permute-start.2
  56.5 26.0 %collective-permute-start.3 = (bf16[16,64,512]{2,1,0:T(8,128)(2,1)S(1)}, bf16[16,64,512]{2,1,0:T(8,128)(2,1)S(1)}, u32[]{:S(2)}, u32[]{:S(2)}) collective-permute-start(bf16[16,64,512]{2,1,0:T(8,128)(2,1)S(1)} %constant_dynamic-update-slice_fusion), channel_id=1, source_target_pairs={{0,16},{8,24},{16,0},{24,8},{1,17},{9,25},{17,1},{25,9},{2,18},{10... | collective-permute-start | bytes 3145736 | tf_op jit(solution)/shard_map/ppermute | solution.py:207
  58.3 45.8 %collective-permute-start.4 = (bf16[16,64,512]{2,1,0:T(8,128)(2,1)S(1)}, bf16[16,64,512]{2,1,0:T(8,128)(2,1)S(1)}, u32[]{:S(2)}, u32[]{:S(2)}) collective-permute-start(bf16[16,64,512]{2,1,0:T(8,128)(2,1)S(1)} %constant_dynamic-update-slice_fusion), channel_id=1, source_target_pairs={{0,24},{8,16},{16,8},{24,0},{1,25},{9,17},{17,9},{25,1},{2,26},{10... | collective-permute-start | bytes 3145736 | tf_op jit(solution)/shard_map/ppermute | solution.py:207
  229.3 3.0 collective-permute-start.6
  230.5 3.6 collective-permute-start.5
  237.5 17.5 %collective-permute-start.7 = (bf16[2,64,2176]{2,1,0:T(8,128)(2,1)S(1)}, bf16[2,64,2176]{2,1,0:T(8,128)(2,1)}, u32[]{:S(2)}, u32[]{:S(2)}) collective-permute-start(bf16[2,64,2176]{2,1,0:T(8,128)(2,1)S(1)} %get-tuple-element.53), channel_id=1, source_target_pairs={{0,16},{8,24},{16,0},{24,8},{1,17},{9,25},{17,1},{25,9},{2,18},{10... | collective-permute-start | bytes 1671176 | tf_op jit(solution)/shard_map/ppermute | solution.py:242
  254.4 17.2 %collective-permute-start.8 = (bf16[2,2,64,2176]{3,2,0,1:T(8,128)(2,1)}, bf16[2,2,64,2176]{3,2,0,1:T(8,128)(2,1)}, u32[]{:S(2)}, u32[]{:S(2)}) collective-permute-start(bf16[2,2,64,2176]{3,2,0,1:T(8,128)(2,1)} %copy.49), channel_id=1, source_target_pairs={{0,8},{8,0},{16,24},{24,16},{1,9},{9,1},{17,25},{25,17},{2,10},{10... | collective-permute-start | bytes 3342344 | tf_op jit(solution)/shard_map/ppermute | solution.py:254
  254.4 19.6 %collective-permute-start.9 = (bf16[2,64,2176]{2,1,0:T(8,128)(2,1)}, bf16[2,64,2176]{2,1,0:T(8,128)(2,1)S(1)}, u32[]{:S(2)}, u32[]{:S(2)}) collective-permute-start(bf16[2,64,2176]{2,1,0:T(8,128)(2,1)} %get-tuple-element.60), channel_id=1, source_target_pairs={{0,16},{8,24},{16,0},{24,8},{1,17},{9,25},{17,1},{25,9},{2,18},{10... | collective-permute-start | bytes 1671176 | tf_op jit(solution)/shard_map/ppermute | solution.py:242
  269.3 21.6 %collective-permute-start.10 = (bf16[2,2,64,2176]{3,2,0,1:T(8,128)(2,1)S(1)}, bf16[2,2,64,2176]{3,2,0,1:T(8,128)(2,1)}, u32[]{:S(2)}, u32[]{:S(2)}) collective-permute-start(bf16[2,2,64,2176]{3,2,0,1:T(8,128)(2,1)S(1)} %copy.52), channel_id=1, source_target_pairs={{0,8},{8,0},{16,24},{24,16},{1,9},{9,1},{17,25},{25,17},{2,10},{10... | collective-permute-start | bytes 3342344 | tf_op jit(solution)/shard_map/ppermute | solution.py:254
  274.0 19.1 %collective-permute-start.11 = (bf16[2,64,2176]{2,1,0:T(8,128)(2,1)}, bf16[2,64,2176]{2,1,0:T(8,128)(2,1)}, u32[]{:S(2)}, u32[]{:S(2)}) collective-permute-start(bf16[2,64,2176]{2,1,0:T(8,128)(2,1)} %get-tuple-element.67), channel_id=1, source_target_pairs={{0,16},{8,24},{16,0},{24,8},{1,17},{9,25},{17,1},{25,9},{2,18},{10... | collective-permute-start | bytes 1671176 | tf_op jit(solution)/shard_map/ppermute | solution.py:242
  290.8 19.2 %collective-permute-start.12 = (bf16[2,2,64,2176]{3,2,0,1:T(8,128)(2,1)}, bf16[2,2,64,2176]{3,2,0,1:T(8,128)(2,1)}, u32[]{:S(2)}, u32[]{:S(2)}) collective-permute-start(bf16[2,2,64,2176]{3,2,0,1:T(8,128)(2,1)} %copy.55), channel_id=1, source_target_pairs={{0,8},{8,0},{16,24},{24,16},{1,9},{9,1},{17,25},{25,17},{2,10},{10... | collective-permute-start | bytes 3342344 | tf_op jit(solution)/shard_map/ppermute | solution.py:254
  292.5 19.9 %collective-permute-start.13 = (bf16[2,64,2176]{2,1,0:T(8,128)(2,1)S(1)}, bf16[2,64,2176]{2,1,0:T(8,128)(2,1)S(1)}, u32[]{:S(2)}, u32[]{:S(2)}) collective-permute-start(bf16[2,64,2176]{2,1,0:T(8,128)(2,1)S(1)} %get-tuple-element.74), channel_id=1, source_target_pairs={{0,16},{8,24},{16,0},{24,8},{1,17},{9,25},{17,1},{25,9},{2,18},{10... | collective-permute-start | bytes 1671176 | tf_op jit(solution)/shard_map/ppermute | solution.py:242
  308.6 20.7 %collective-permute-start.14 = (bf16[2,2,64,2176]{3,2,0,1:T(8,128)(2,1)}, bf16[2,2,64,2176]{3,2,0,1:T(8,128)(2,1)}, u32[]{:S(2)}, u32[]{:S(2)}) collective-permute-start(bf16[2,2,64,2176]{3,2,0,1:T(8,128)(2,1)} %copy.58), channel_id=1, source_target_pairs={{0,8},{8,0},{16,24},{24,16},{1,9},{9,1},{17,25},{25,17},{2,10},{10... | collective-permute-start | bytes 3342344 | tf_op jit(solution)/shard_map/ppermute | solution.py:254
  312.4 19.8 %collective-permute-start.15 = (bf16[2,64,2176]{2,1,0:T(8,128)(2,1)}, bf16[2,64,2176]{2,1,0:T(8,128)(2,1)}, u32[]{:S(2)}, u32[]{:S(2)}) collective-permute-start(bf16[2,64,2176]{2,1,0:T(8,128)(2,1)} %get-tuple-element.81), channel_id=1, source_target_pairs={{0,16},{8,24},{16,0},{24,8},{1,17},{9,25},{17,1},{25,9},{2,18},{10... | collective-permute-start | bytes 1671176 | tf_op jit(solution)/shard_map/ppermute | solution.py:242
  329.1 19.0 %collective-permute-start.17 = (bf16[2,2,64,2176]{3,2,0,1:T(8,128)(2,1)}, bf16[2,2,64,2176]{3,2,0,1:T(8,128)(2,1)S(1)}, u32[]{:S(2)}, u32[]{:S(2)}) collective-permute-start(bf16[2,2,64,2176]{3,2,0,1:T(8,128)(2,1)} %copy.61), channel_id=1, source_target_pairs={{0,8},{8,0},{16,24},{24,16},{1,9},{9,1},{17,25},{25,17},{2,10},{10... | collective-permute-start | bytes 3342344 | tf_op jit(solution)/shard_map/ppermute | solution.py:254
  331.7 18.2 %collective-permute-start.16 = (bf16[2,64,2176]{2,1,0:T(8,128)(2,1)}, bf16[2,64,2176]{2,1,0:T(8,128)(2,1)S(1)}, u32[]{:S(2)}, u32[]{:S(2)}) collective-permute-start(bf16[2,64,2176]{2,1,0:T(8,128)(2,1)} %get-tuple-element.84), channel_id=1, source_target_pairs={{0,16},{8,24},{16,0},{24,8},{1,17},{9,25},{17,1},{25,9},{2,18},{10... | collective-permute-start | bytes 1671176 | tf_op jit(solution)/shard_map/ppermute | solution.py:242
  346.6 3.3 collective-permute-start.19
  348.3 15.5 %collective-permute-start.18 = (bf16[2,64,2176]{2,1,0:T(8,128)(2,1)S(1)}, bf16[2,64,2176]{2,1,0:T(8,128)(2,1)S(1)}, u32[]{:S(2)}, u32[]{:S(2)}) collective-permute-start(bf16[2,64,2176]{2,1,0:T(8,128)(2,1)S(1)} %fusion.12), channel_id=1, source_target_pairs={{0,16},{8,24},{16,0},{24,8},{1,17},{9,25},{17,1},{25,9},{2,18},{10... | collective-permute-start | bytes 1671176 | tf_op jit(solution)/shard_map/ppermute | solution.py:242
  350.1 25.0 %collective-permute-start.20 = (bf16[2,64,2176]{2,1,0:T(8,128)(2,1)S(1)}, bf16[2,64,2176]{2,1,0:T(8,128)(2,1)S(1)}, u32[]{:S(2)}, u32[]{:S(2)}) collective-permute-start(bf16[2,64,2176]{2,1,0:T(8,128)(2,1)S(1)} %fusion.13), channel_id=1, source_target_pairs={{0,16},{8,24},{16,0},{24,8},{1,17},{9,25},{17,1},{25,9},{2,18},{10... | collective-permute-start | bytes 1671176 | tf_op jit(solution)/shard_map/ppermute | solution.py:242
  (5 other events, 9.1 us)
Sparse Core Ops, SparseCore 0:
  11.3 165.8 all-gather.2

commit v4 on v3

--- a/solution.py
+++ b/solution.py
@@ -75,30 +75,46 @@
         out_ref[start : start + group, 0, :, width + FLAG_LANES :] = moved[:, :, width:]
 
 
-def dispatch(first, lists, rows, owned, cap, cluster_count):
+def dispatch(first, lists, rows, owned, cap, cluster_count, number, held):
     sources, picks, count = lists.shape
     total = rows.shape[2] + FLAG_LANES
+    kernel = functools.partial(dispatch_kernel, cluster_count)
+    in_specs = [
+        pl.BlockSpec(memory_space=pltpu.SMEM),
+        pl.BlockSpec((sources, picks, count), lambda s: (0, 0, 0)),
+        pl.BlockSpec((1, count, rows.shape[2]), lambda s: (s, 0, 0)),
+    ]
+    operands = [first, lists, rows]
+    aliases = {}
+    body = kernel
+    if held is not None:
+        in_specs.append(pl.BlockSpec(memory_space=pl.ANY))
+        operands.append(held)
+        aliases = {3: 0}
+
+        def body(first_ref, lists_ref, rows_ref, held_ref, out_ref, rank_ref, hit_ref):
+            kernel(first_ref, lists_ref, rows_ref, out_ref, rank_ref, hit_ref)
+
     return pl.pallas_call(
-        functools.partial(dispatch_kernel, cluster_count),
+        body,
         grid=(sources,),
-        in_specs=[
-            pl.BlockSpec(memory_space=pltpu.SMEM),
-            pl.BlockSpec((sources, picks, count), lambda s: (0, 0, 0)),
-            pl.BlockSpec((1, count, rows.shape[2]), lambda s: (s, 0, 0)),
-        ],
-        out_specs=pl.BlockSpec((owned, 1, cap, total), lambda s: (0, s, 0, 0)),
-        out_shape=jax.ShapeDtypeStruct((owned, sources, cap, total), jnp.bfloat16),
+        in_specs=in_specs,
+        out_specs=pl.BlockSpec(
+            (owned, 1, cap, total), lambda s: (0, s + number * sources, 0, 0)
+        ),
+        out_shape=jax.ShapeDtypeStruct((owned, 2 * sources, cap, total), jnp.bfloat16),
         scratch_shapes=[
             pltpu.VMEM((sources, owned, count), jnp.int32),
             pltpu.VMEM((sources, FLAG_LANES, count), jnp.bfloat16),
         ],
+        input_output_aliases=aliases,
         compiler_params=pltpu.CompilerParams(vmem_limit_bytes=48 * 2**20),
         cost_estimate=pl.CostEstimate(
             flops=2 * sources * owned * cap * count * total,
             bytes_accessed=2 * sources * (count * rows.shape[2] + owned * cap * total),
             transcendentals=0,
         ),
-    )(first, lists, rows)
+    )(*operands)
 
 
 def block_kernel(base, near_count, scale, spots_ref, slots_ref, marks_ref, keep_ref, send_ref):
@@ -189,9 +205,29 @@
     listed = jnp.pad(cluster_lists.T.astype(jnp.bfloat16), ((0, 0), (0, per_pick * lanes - count)))
     listed = listed.reshape(picks * per_pick, lanes)
     listed = jnp.pad(listed, ((0, -(picks * per_pick) % 16), (0, 0)))
-    all_rows = lax.all_gather(jnp.concatenate([rows, listed], axis=0), "lmk")
-    all_lists = all_rows[:, count : count + picks * per_pick].reshape(lmk_count, picks, -1)
-    all_lists = all_lists[:, :, :count].astype(jnp.int32)
+    own = jnp.concatenate([rows, listed], axis=0)
+    inner = lmk_count // 4
+
+    def shifted(data, outer):
+        return lax.ppermute(data, "lmk", [(i, i ^ (outer * inner)) for i in range(lmk_count)])
+
+    def spread(data):
+        gathered = [data]
+        for turn in range(1, inner):
+            pairs = [(i, i - i % inner + (i % inner + turn) % inner) for i in range(lmk_count)]
+            gathered.append(lax.ppermute(data, "lmk", pairs))
+        return gathered
+
+    near_z = shifted(own, 1)
+    far_z = shifted(own, 2)
+    halves = [
+        jnp.stack(spread(own) + spread(near_z)),
+        jnp.stack(spread(far_z) + spread(shifted(near_z, 2))),
+    ]
+
+    def lists_of(half):
+        taken = half[:, count : count + picks * per_pick].reshape(half.shape[0], picks, -1)
+        return taken[:, :, :count].astype(jnp.int32)
 
     forward = [(i, (i + 1) % lmk_count) for i in range(lmk_count)]
     backward = [(target, source) for source, target in forward]
@@ -224,9 +260,18 @@
     my_part = my_cmp // 2
     spots = jnp.concatenate([spots, my_core[None]]).astype(jnp.int32)
 
-    slots = dispatch(
-        jnp.asarray(first, jnp.int32)[None], all_lists, all_rows, owned, cap, cluster_count
-    )
+    slots = None
+    for number, half in enumerate(halves):
+        slots = dispatch(
+            jnp.asarray(first, jnp.int32)[None],
+            lists_of(half),
+            half,
+            owned,
+            cap,
+            cluster_count,
+            number,
+            slots,
+        )
     slots = slots.reshape(owned, lmk_count * cap, slots.shape[3])
     parts = cmp_count // 2
     cores = [(i, i ^ 1) for i in range(cmp_count)]

time: 398 us -> 412 us (1.035)
  between operations: 14.8 us -> 1.35 us
  starting transfers between devices: 18.3 us -> 29.4 us
  local copies, waits for them, and re-layouts: 23.9 us -> 34.7 us
  other arithmetic: 33.4 us -> 39.9 us
    ppermute x0 -> x7, waiting for transfers between devices: none -> 124 us  [the longest x3 90.3 us: shifted(): lax.ppermute(data, 'lmk', [(i, i ^ outer * inner) for i in range(lmk_coun...]
    all_gather x1 -> x0, waiting for transfers between devices: 62.2 us -> none  [on_device(): all_rows = lax.all_gather(jnp.concatenate([rows, listed], axis=0), 'lmk')]
    ppermute x3, waiting for transfers between devices: 44.5 us -> 0.01 us  [on_device(): piece = lax.ppermute(rims, 'cmp', swap) if turn else rims]
    ppermute x1, waiting for transfers between devices: 28.5 us -> 15.6 us  [on_device(): low = lax.ppermute(quarter[owned - rim:], 'lmk', forward)]
    ppermute x0 -> x7, starting transfers between devices: none -> 11.7 us  [the longest x4 9.99 us: spread(): gathered.append(lax.ppermute(data, 'lmk', pairs))]
    unnamed x18 -> x28, local copies, waits for them, and re-layouts: 14.2 us -> 22.4 us
    another operation x0 -> x3, other arithmetic: none -> 8.07 us  [the longest x2 4.89 us: on_device(): jnp.stack(spread(own) + spread(near_z))]
    pallas_call x1 -> x2, Pallas kernels: 22.6 us -> 22.8 us  [dispatch(): pl.pallas_call(body, grid=(sources,), in_specs=in_specs, out_specs=pl.Blo...]
  transfers between devices with their start and end apart: 22 -> 28, of which waited for: 9 -> 9; matrix products, arithmetic and copies ran while one was open for 9% -> 9% of each run, Pallas kernels for 22% -> 24%
where the time goes in v4:
time: 412 us; the launch traced here: 408 us
  waiting for transfers between devices  166 us (40%)
  Pallas kernels  137 us (33%)
  other arithmetic  39.9 us (10%)
  local copies, waits for them, and re-layouts  34.7 us (8%)
  starting transfers between devices  29.4 us (7%)
    pallas_call x8, Pallas kernels, blocks(): pl.pallas_call(functools.partial(block_kernel, base, near_count, scale),...  114 us
    ppermute x3, waiting for transfers between devices, shifted(): lax.ppermute(data, 'lmk', [(i, i ^ outer * inner) for i in range(lmk_coun...  90.3 us
    ppermute x4, waiting for transfers between devices, spread(): gathered.append(lax.ppermute(data, 'lmk', pairs))  33.5 us
    ppermute x8, waiting for transfers between devices, cross(): pieces.append(lax.ppermute(sums[hop], 'cmp', across))  23.1 us
    pallas_call x2, Pallas kernels, dispatch(): pl.pallas_call(body, grid=(sources,), in_specs=in_specs, out_specs=pl.Blo...  22.8 us
    unnamed x28, local copies, waits for them, and re-layouts  22.4 us
    ppermute x1, waiting for transfers between devices, on_device(): low = lax.ppermute(quarter[owned - rim:], 'lmk', forward)  15.6 us
    convert_element_type x7, other arithmetic, on_device(): sums.append(mine.astype(jnp.bfloat16) if hop else mine)  11.7 us
  transfers between devices with their start and end apart: 28, of which 9 were waited for; matrix products, arithmetic and copies ran while one was open for 9% of the time, Pallas kernels for 24%

profile of v4, /device:TPU:0, one launch (start us, length us, event | category | flops | bytes accessed | tf_op | source)
XLA Modules:
  0.0 407.8 jit_solution(16737817146886325420)
XLA Ops:
  0.6 3.2 fusion
  8.9 6.0 %collective-permute-start.8 = (bf16[8,64,512]{2,1,0:T(8,128)(2,1)}, bf16[8,64,512]{2,1,0:T(8,128)(2,1)S(1)}, u32[]{:S(2)}, u32[]{:S(2)}) collective-permute-start(bf16[8,64,512]{2,1,0:T(8,128)(2,1)} %get-tuple-element.96), channel_id=1, source_target_pairs={{1,0},{2,1},{3,2},{4,3},{5,4},{6,5},{7,6},{0,7},{9,8},{10,9},{11,1... | collective-permute-start | bytes 1572872 | tf_op jit(solution)/shard_map/ppermute | solution.py:238
  19.8 15.6 %collective-permute-done.7 = bf16[8,64,512]{2,1,0:T(8,128)(2,1)S(1)} collective-permute-done((bf16[8,64,512]{2,1,0:T(8,128)(2,1)}, bf16[8,64,512]{2,1,0:T(8,128)(2,1)S(1)}, u32[]{:S(2)}, u32[]{:S(2)}) %collective-permute-start.7) | collective-permute-done | bytes 524320 | tf_op jit(solution)/shard_map/ppermute | solution.py:237
  38.5 43.9 %collective-permute-done.2 = bf16[1040,640]{1,0:T(8,128)(2,1)} collective-permute-done((bf16[1040,640]{1,0:T(8,128)(2,1)}, bf16[1040,640]{1,0:T(8,128)(2,1)}, u32[]{:S(2)}, u32[]{:S(2)}) %collective-permute-start.2) | collective-permute-done | bytes 1331232 | tf_op jit(solution)/shard_map/ppermute | solution.py:212
  82.4 6.2 %collective-permute-start.5 = (bf16[1040,640]{1,0:T(8,128)(2,1)}, bf16[1040,640]{1,0:T(8,128)(2,1)S(1)}, u32[]{:S(2)}, u32[]{:S(2)}) collective-permute-start(bf16[1040,640]{1,0:T(8,128)(2,1)} %get-tuple-element.111), channel_id=1, source_target_pairs={{0,1},{1,0},{2,3},{3,2},{4,5},{5,4},{6,7},{7,6},{8,9},{9,8},{10,11... | collective-permute-start | bytes 3993608 | tf_op jit(solution)/shard_map/ppermute | solution.py:218
  94.5 8.3 %pad_maximum_fusion.marks_ref = bf16[32,256,640]{2,1,0:T(8,128)(2,1)} fusion(bf16[32,256,128]{2,1,0:T(8,128)(2,1)S(1)} %broadcast_in_dim.48, bf16[8,256,512]{2,1,0:T(8,128)(2,1)S(1)} %bitcast.103, bf16[16,256,512]{2,1,0:T(8,128)(2,1)S(1)} %copy-done.4, bf16[8,256,512]{2,1,0:T(8,128)(2,1)S(1)} %bitcast.102), kind=kLoop, calls=%fused_computation.2 | loop fusion | flops 41943040 | bytes 20971520 | tf_op jit(solution)/shard_map/concatenate | solution.py:255
  102.8 46.3 %collective-permute-done.3 = bf16[1040,640]{1,0:T(8,128)(2,1)} collective-permute-done((bf16[1040,640]{1,0:T(8,128)(2,1)}, bf16[1040,640]{1,0:T(8,128)(2,1)}, u32[]{:S(2)}, u32[]{:S(2)}) %collective-permute-start.3) | collective-permute-done | bytes 1331232 | tf_op jit(solution)/shard_map/ppermute | solution.py:212
  158.5 11.4 %shard_map.68.held_ref = bf16[16,8,64,768]{3,2,1,0:T(8,128)(2,1)} custom-call(s32[1]{0:T(128)} %bitcast.1.first_ref, s32[4,4,1024]{2,1,0:T(4,128)S(1)} %slice_convert_fusion.lists_ref, bf16[4,1040,640]{2,1,0:T(8,128)(2,1)S(1)} %copy-done.3), custom_call_target="tpu_custom_call" | custom-call | flops 6442450944 | bytes 11534336 | tf_op jit(solution)/shard_map/pallas_call | solution.py:98
  169.9 6.1 %collective-permute-done.1 = bf16[1040,640]{1,0:T(8,128)(2,1)} collective-permute-done((bf16[1040,640]{1,0:T(8,128)(2,1)}, bf16[1040,640]{1,0:T(8,128)(2,1)}, u32[]{:S(2)}, u32[]{:S(2)}) %collective-permute-start.1) | collective-permute-done | bytes 1331232 | tf_op jit(solution)/shard_map/ppermute | solution.py:218
  176.0 27.3 %collective-permute-done.4 = bf16[1040,640]{1,0:T(8,128)(2,1)S(1)} collective-permute-done((bf16[1040,640]{1,0:T(8,128)(2,1)}, bf16[1040,640]{1,0:T(8,128)(2,1)S(1)}, u32[]{:S(2)}, u32[]{:S(2)}) %collective-permute-start.4) | collective-permute-done | bytes 1331232 | tf_op jit(solution)/shard_map/ppermute | solution.py:218
  203.3 3.2 pad_maximum_fusion.1.rows_ref
  211.5 11.4 %shard_map.69 = bf16[16,8,64,768]{3,2,1,0:T(8,128)(2,1)} custom-call(s32[1]{0:T(128)} %bitcast.1.first_ref, s32[4,4,1024]{2,1,0:T(4,128)S(1)} %slice_convert_fusion.1.lists_ref, bf16[4,1040,640]{2,1,0:T(8,128)(2,1)S(1)} %copy-done.1, bf16[16,8,64,768]{3,2,1,0:T(8,128)(2,1)} %shard_map.68.held_ref), custom_call_target="tpu_custom_call", output_to_operand_aliasing={{}: (3, {})} | custom-call | flops 6442450944 | bytes 11534336 | tf_op jit(solution)/shard_map/pallas_call | solution.py:98
  222.9 14.1 %shard_map.71 = (bf16[2,2,64,2176]{3,2,1,0:T(8,128)(2,1)S(1)}, bf16[2,2,64,2176]{3,2,1,0:T(8,128)(2,1)S(1)}) custom-call(s32[129]{0:T(256)S(1)} %pad_add_fusion.spots_ref, bf16[16,512,768]{2,1,0:T(8,128)(2,1)} %bitcast.92, bf16[32,256,640]{2,1,0:T(8,128)(2,1)} %pad_maximum_fusion.marks_ref), custom_call_target="tpu_custom_call" | custom-call | flops 1048576 | bytes 1048576 | tf_op jit(solution)/shard_map/pallas_call | solution.py:169
  237.0 14.4 %shard_map.70 = (bf16[2,2,64,2176]{3,2,1,0:T(8,128)(2,1)S(1)}, bf16[2,2,64,2176]{3,2,1,0:T(8,128)(2,1)S(1)}) custom-call(s32[129]{0:T(256)S(1)} %pad_add_fusion.spots_ref, bf16[16,512,768]{2,1,0:T(8,128)(2,1)} %bitcast.93, bf16[32,256,640]{2,1,0:T(8,128)(2,1)} %pad_maximum_fusion.marks_ref), custom_call_target="tpu_custom_call" | custom-call | flops 1048576 | bytes 1048576 | tf_op jit(solution)/shard_map/pallas_call | solution.py:169
  260.8 14.1 %shard_map.72 = (bf16[2,2,64,2176]{3,2,1,0:T(8,128)(2,1)S(1)}, bf16[2,2,64,2176]{3,2,1,0:T(8,128)(2,1)S(1)}) custom-call(s32[129]{0:T(256)S(1)} %pad_add_fusion.spots_ref, bf16[16,512,768]{2,1,0:T(8,128)(2,1)} %bitcast.94, bf16[32,256,640]{2,1,0:T(8,128)(2,1)} %pad_maximum_fusion.marks_ref), custom_call_target="tpu_custom_call" | custom-call | flops 1048576 | bytes 1048576 | tf_op jit(solution)/shard_map/pallas_call | solution.py:169
  276.5 14.3 %shard_map.73 = (bf16[2,2,64,2176]{3,2,1,0:T(8,128)(2,1)S(1)}, bf16[2,2,64,2176]{3,2,1,0:T(8,128)(2,1)S(1)}) custom-call(s32[129]{0:T(256)S(1)} %pad_add_fusion.spots_ref, bf16[16,512,768]{2,1,0:T(8,128)(2,1)} %bitcast.95, bf16[32,256,640]{2,1,0:T(8,128)(2,1)} %pad_maximum_fusion.marks_ref), custom_call_target="tpu_custom_call" | custom-call | flops 1048576 | bytes 1048576 | tf_op jit(solution)/shard_map/pallas_call | solution.py:169
  296.2 14.5 %shard_map.74 = (bf16[2,2,64,2176]{3,2,1,0:T(8,128)(2,1)S(1)}, bf16[2,2,64,2176]{3,2,1,0:T(8,128)(2,1)S(1)}) custom-call(s32[129]{0:T(256)S(1)} %pad_add_fusion.spots_ref, bf16[16,512,768]{2,1,0:T(8,128)(2,1)} %bitcast.96, bf16[32,256,640]{2,1,0:T(8,128)(2,1)} %pad_maximum_fusion.marks_ref), custom_call_target="tpu_custom_call" | custom-call | flops 1048576 | bytes 1048576 | tf_op jit(solution)/shard_map/pallas_call | solution.py:169
  315.1 14.1 %shard_map.75 = (bf16[2,2,64,2176]{3,2,1,0:T(8,128)(2,1)S(1)}, bf16[2,2,64,2176]{3,2,1,0:T(8,128)(2,1)S(1)}) custom-call(s32[129]{0:T(256)S(1)} %pad_add_fusion.spots_ref, bf16[16,512,768]{2,1,0:T(8,128)(2,1)} %bitcast.97, bf16[32,256,640]{2,1,0:T(8,128)(2,1)} %pad_maximum_fusion.marks_ref), custom_call_target="tpu_custom_call" | custom-call | flops 1048576 | bytes 1048576 | tf_op jit(solution)/shard_map/pallas_call | solution.py:169
  335.6 14.1 %shard_map.76 = (bf16[2,2,64,2176]{3,2,1,0:T(8,128)(2,1)S(1)}, bf16[2,2,64,2176]{3,2,1,0:T(8,128)(2,1)S(1)}) custom-call(s32[129]{0:T(256)S(1)} %pad_add_fusion.spots_ref, bf16[16,512,768]{2,1,0:T(8,128)(2,1)} %bitcast.98, bf16[32,256,640]{2,1,0:T(8,128)(2,1)} %pad_maximum_fusion.marks_ref), custom_call_target="tpu_custom_call" | custom-call | flops 1048576 | bytes 1048576 | tf_op jit(solution)/shard_map/pallas_call | solution.py:169
  353.8 14.3 %shard_map.77 = (bf16[2,2,64,2176]{3,2,1,0:T(8,128)(2,1)S(1)}, bf16[2,2,64,2176]{3,2,1,0:T(8,128)(2,1)S(1)}) custom-call(s32[129]{0:T(256)S(1)} %pad_add_fusion.spots_ref, bf16[16,512,768]{2,1,0:T(8,128)(2,1)} %bitcast.99, bf16[32,256,640]{2,1,0:T(8,128)(2,1)} %pad_maximum_fusion.marks_ref), custom_call_target="tpu_custom_call" | custom-call | flops 1048576 | bytes 1048576 | tf_op jit(solution)/shard_map/pallas_call | solution.py:169
  373.3 12.0 %collective-permute-done.25 = bf16[2,64,2176]{2,1,0:T(8,128)(2,1)S(1)} collective-permute-done((bf16[2,64,2176]{2,1,0:T(8,128)(2,1)S(1)}, bf16[2,64,2176]{2,1,0:T(8,128)(2,1)S(1)}, u32[]{:S(2)}, u32[]{:S(2)}) %collective-permute-start.25) | collective-permute-done | bytes 557088 | tf_op jit(solution)/shard_map/ppermute | solution.py:287
  385.5 11.1 %collective-permute-done.27 = bf16[2,64,2176]{2,1,0:T(8,128)(2,1)S(1)} collective-permute-done((bf16[2,64,2176]{2,1,0:T(8,128)(2,1)S(1)}, bf16[2,64,2176]{2,1,0:T(8,128)(2,1)S(1)}, u32[]{:S(2)}, u32[]{:S(2)}) %collective-permute-start.27) | collective-permute-done | bytes 557088 | tf_op jit(solution)/shard_map/ppermute | solution.py:287
  398.0 4.1 %copy.69 = f32[128,8,8,256]{3,2,1,0:T(8,128)S(1)} copy(f32[128,8,8,256]{3,1,2,0:T(8,128)S(1)} %bitcast.100) | data formatting | bytes 16777216
  402.1 4.4 %copy.66 = f32[64,16,8,256]{3,2,1,0:T(8,128)} copy(f32[64,16,8,256]{3,2,0,1:T(8,128)S(1)} %bitcast.101) | data formatting | bytes 16777216
  (127 shorter events, 71.7 us)
Async XLA Ops:
  8.9 26.6 %collective-permute-start.8 = (bf16[8,64,512]{2,1,0:T(8,128)(2,1)}, bf16[8,64,512]{2,1,0:T(8,128)(2,1)S(1)}, u32[]{:S(2)}, u32[]{:S(2)}) collective-permute-start(bf16[8,64,512]{2,1,0:T(8,128)(2,1)} %get-tuple-element.96), channel_id=1, source_target_pairs={{1,0},{2,1},{3,2},{4,3},{5,4},{6,5},{7,6},{0,7},{9,8},{10,9},{11,1... | collective-permute-start | bytes 1572872 | tf_op jit(solution)/shard_map/ppermute | solution.py:238
  14.9 20.6 %collective-permute-start.7 = (bf16[8,64,512]{2,1,0:T(8,128)(2,1)}, bf16[8,64,512]{2,1,0:T(8,128)(2,1)S(1)}, u32[]{:S(2)}, u32[]{:S(2)}) collective-permute-start(bf16[8,64,512]{2,1,0:T(8,128)(2,1)} %get-tuple-element.97), channel_id=1, source_target_pairs={{0,1},{1,2},{2,3},{3,4},{4,5},{5,6},{6,7},{7,0},{8,9},{9,10},{10,1... | collective-permute-start | bytes 1572872 | tf_op jit(solution)/shard_map/ppermute | solution.py:237
  18.2 64.2 %collective-permute-start.2 = (bf16[1040,640]{1,0:T(8,128)(2,1)}, bf16[1040,640]{1,0:T(8,128)(2,1)}, u32[]{:S(2)}, u32[]{:S(2)}) collective-permute-start(bf16[1040,640]{1,0:T(8,128)(2,1)} %get-tuple-element.111), channel_id=1, source_target_pairs={{0,2},{1,3},{2,0},{3,1},{4,6},{5,7},{6,4},{7,5},{8,10},{9,11},{10,... | collective-permute-start | bytes 3993608 | tf_op jit(solution)/shard_map/ppermute | solution.py:212
  18.2 71.7 %collective-permute-start = (bf16[1040,640]{1,0:T(8,128)(2,1)}, bf16[1040,640]{1,0:T(8,128)(2,1)}, u32[]{:S(2)}, u32[]{:S(2)}) collective-permute-start(bf16[1040,640]{1,0:T(8,128)(2,1)} %get-tuple-element.111), channel_id=1, source_target_pairs={{0,4},{1,5},{2,6},{3,7},{4,0},{5,1},{6,2},{7,3},{8,12},{9,13},{10,... | collective-permute-start | bytes 3993608 | tf_op jit(solution)/shard_map/ppermute | solution.py:212
  35.6 53.0 %collective-permute-start.9 = (bf16[16,64,512]{2,1,0:T(8,128)(2,1)S(1)}, bf16[16,64,512]{2,1,0:T(8,128)(2,1)}, u32[]{:S(2)}, u32[]{:S(2)}) collective-permute-start(bf16[16,64,512]{2,1,0:T(8,128)(2,1)S(1)} %constant_dynamic-update-slice_fusion), channel_id=1, source_target_pairs={{0,8},{8,0},{16,24},{24,16},{1,9},{9,1},{17,25},{25,17},{2,10},{10... | collective-permute-start | bytes 3145736 | tf_op jit(solution)/shard_map/ppermute | solution.py:243
  35.7 54.4 %collective-permute-start.10 = (bf16[16,64,512]{2,1,0:T(8,128)(2,1)S(1)}, bf16[16,64,512]{2,1,0:T(8,128)(2,1)S(1)}, u32[]{:S(2)}, u32[]{:S(2)}) collective-permute-start(bf16[16,64,512]{2,1,0:T(8,128)(2,1)S(1)} %constant_dynamic-update-slice_fusion), channel_id=1, source_target_pairs={{0,16},{8,24},{16,0},{24,8},{1,17},{9,25},{17,1},{25,9},{2,18},{10... | collective-permute-start | bytes 3145736 | tf_op jit(solution)/shard_map/ppermute | solution.py:243
  37.5 54.7 %collective-permute-start.11 = (bf16[16,64,512]{2,1,0:T(8,128)(2,1)S(1)}, bf16[16,64,512]{2,1,0:T(8,128)(2,1)S(1)}, u32[]{:S(2)}, u32[]{:S(2)}) collective-permute-start(bf16[16,64,512]{2,1,0:T(8,128)(2,1)S(1)} %constant_dynamic-update-slice_fusion), channel_id=1, source_target_pairs={{0,24},{8,16},{16,8},{24,0},{1,25},{9,17},{17,9},{25,1},{2,26},{10... | collective-permute-start | bytes 3145736 | tf_op jit(solution)/shard_map/ppermute | solution.py:243
  82.4 68.5 %collective-permute-start.5 = (bf16[1040,640]{1,0:T(8,128)(2,1)}, bf16[1040,640]{1,0:T(8,128)(2,1)S(1)}, u32[]{:S(2)}, u32[]{:S(2)}) collective-permute-start(bf16[1040,640]{1,0:T(8,128)(2,1)} %get-tuple-element.111), channel_id=1, source_target_pairs={{0,1},{1,0},{2,3},{3,2},{4,5},{5,4},{6,7},{7,6},{8,9},{9,8},{10,11... | collective-permute-start | bytes 3993608 | tf_op jit(solution)/shard_map/ppermute | solution.py:218
  88.6 62.3 %collective-permute-start.6 = (bf16[1040,640]{1,0:T(8,128)(2,1)}, bf16[1040,640]{1,0:T(8,128)(2,1)S(1)}, u32[]{:S(2)}, u32[]{:S(2)}) collective-permute-start(bf16[1040,640]{1,0:T(8,128)(2,1)} %collective-permute-done.2), channel_id=1, source_target_pairs={{0,1},{1,0},{2,3},{3,2},{4,5},{5,4},{6,7},{7,6},{8,9},{9,8},{10,11... | collective-permute-start | bytes 3993608 | tf_op jit(solution)/shard_map/ppermute | solution.py:218
  89.9 59.2 %collective-permute-start.3 = (bf16[1040,640]{1,0:T(8,128)(2,1)}, bf16[1040,640]{1,0:T(8,128)(2,1)}, u32[]{:S(2)}, u32[]{:S(2)}) collective-permute-start(bf16[1040,640]{1,0:T(8,128)(2,1)} %collective-permute-done.2), channel_id=1, source_target_pairs={{0,4},{1,5},{2,6},{3,7},{4,0},{5,1},{6,2},{7,3},{8,12},{9,13},{10,... | collective-permute-start | bytes 3993608 | tf_op jit(solution)/shard_map/ppermute | solution.py:212
  90.0 86.0 %collective-permute-start.1 = (bf16[1040,640]{1,0:T(8,128)(2,1)}, bf16[1040,640]{1,0:T(8,128)(2,1)}, u32[]{:S(2)}, u32[]{:S(2)}) collective-permute-start(bf16[1040,640]{1,0:T(8,128)(2,1)} %collective-permute-done), channel_id=1, source_target_pairs={{0,1},{1,0},{2,3},{3,2},{4,5},{5,4},{6,7},{7,6},{8,9},{9,8},{10,11... | collective-permute-start | bytes 3993608 | tf_op jit(solution)/shard_map/ppermute | solution.py:218
  149.2 54.2 %collective-permute-start.4 = (bf16[1040,640]{1,0:T(8,128)(2,1)}, bf16[1040,640]{1,0:T(8,128)(2,1)S(1)}, u32[]{:S(2)}, u32[]{:S(2)}) collective-permute-start(bf16[1040,640]{1,0:T(8,128)(2,1)} %collective-permute-done.3), channel_id=1, source_target_pairs={{0,1},{1,0},{2,3},{3,2},{4,5},{5,4},{6,7},{7,6},{8,9},{9,8},{10,11... | collective-permute-start | bytes 3993608 | tf_op jit(solution)/shard_map/ppermute | solution.py:218
  259.3 17.3 %collective-permute-start.14 = (bf16[2,64,2176]{2,1,0:T(8,128)(2,1)S(1)}, bf16[2,64,2176]{2,1,0:T(8,128)(2,1)S(1)}, u32[]{:S(2)}, u32[]{:S(2)}) collective-permute-start(bf16[2,64,2176]{2,1,0:T(8,128)(2,1)S(1)} %get-tuple-element.53), channel_id=1, source_target_pairs={{0,16},{8,24},{16,0},{24,8},{1,17},{9,25},{17,1},{25,9},{2,18},{10... | collective-permute-start | bytes 1671176 | tf_op jit(solution)/shard_map/ppermute | solution.py:287
  276.0 16.4 %collective-permute-start.15 = (bf16[2,2,64,2176]{3,2,0,1:T(8,128)(2,1)}, bf16[2,2,64,2176]{3,2,0,1:T(8,128)(2,1)}, u32[]{:S(2)}, u32[]{:S(2)}) collective-permute-start(bf16[2,2,64,2176]{3,2,0,1:T(8,128)(2,1)} %copy.50), channel_id=1, source_target_pairs={{0,8},{8,0},{16,24},{24,16},{1,9},{9,1},{17,25},{25,17},{2,10},{10... | collective-permute-start | bytes 3342344 | tf_op jit(solution)/shard_map/ppermute | solution.py:299
  276.0 18.7 %collective-permute-start.16 = (bf16[2,64,2176]{2,1,0:T(8,128)(2,1)S(1)}, bf16[2,64,2176]{2,1,0:T(8,128)(2,1)}, u32[]{:S(2)}, u32[]{:S(2)}) collective-permute-start(bf16[2,64,2176]{2,1,0:T(8,128)(2,1)S(1)} %get-tuple-element.60), channel_id=1, source_target_pairs={{0,16},{8,24},{16,0},{24,8},{1,17},{9,25},{17,1},{25,9},{2,18},{10... | collective-permute-start | bytes 1671176 | tf_op jit(solution)/shard_map/ppermute | solution.py:287
  291.0 22.0 %collective-permute-start.17 = (bf16[2,2,64,2176]{3,2,0,1:T(8,128)(2,1)S(1)}, bf16[2,2,64,2176]{3,2,0,1:T(8,128)(2,1)}, u32[]{:S(2)}, u32[]{:S(2)}) collective-permute-start(bf16[2,2,64,2176]{3,2,0,1:T(8,128)(2,1)S(1)} %copy.53), channel_id=1, source_target_pairs={{0,8},{8,0},{16,24},{24,16},{1,9},{9,1},{17,25},{25,17},{2,10},{10... | collective-permute-start | bytes 3342344 | tf_op jit(solution)/shard_map/ppermute | solution.py:299
  294.7 20.4 %collective-permute-start.18 = (bf16[2,64,2176]{2,1,0:T(8,128)(2,1)}, bf16[2,64,2176]{2,1,0:T(8,128)(2,1)}, u32[]{:S(2)}, u32[]{:S(2)}) collective-permute-start(bf16[2,64,2176]{2,1,0:T(8,128)(2,1)} %get-tuple-element.67), channel_id=1, source_target_pairs={{0,16},{8,24},{16,0},{24,8},{1,17},{9,25},{17,1},{25,9},{2,18},{10... | collective-permute-start | bytes 1671176 | tf_op jit(solution)/shard_map/ppermute | solution.py:287
  311.8 19.9 %collective-permute-start.19 = (bf16[2,2,64,2176]{3,2,0,1:T(8,128)(2,1)}, bf16[2,2,64,2176]{3,2,0,1:T(8,128)(2,1)}, u32[]{:S(2)}, u32[]{:S(2)}) collective-permute-start(bf16[2,2,64,2176]{3,2,0,1:T(8,128)(2,1)} %copy.56), channel_id=1, source_target_pairs={{0,8},{8,0},{16,24},{24,16},{1,9},{9,1},{17,25},{25,17},{2,10},{10... | collective-permute-start | bytes 3342344 | tf_op jit(solution)/shard_map/ppermute | solution.py:299
  314.5 19.6 %collective-permute-start.20 = (bf16[2,64,2176]{2,1,0:T(8,128)(2,1)S(1)}, bf16[2,64,2176]{2,1,0:T(8,128)(2,1)S(1)}, u32[]{:S(2)}, u32[]{:S(2)}) collective-permute-start(bf16[2,64,2176]{2,1,0:T(8,128)(2,1)S(1)} %get-tuple-element.74), channel_id=1, source_target_pairs={{0,16},{8,24},{16,0},{24,8},{1,17},{9,25},{17,1},{25,9},{2,18},{10... | collective-permute-start | bytes 1671176 | tf_op jit(solution)/shard_map/ppermute | solution.py:287
  330.3 20.6 %collective-permute-start.21 = (bf16[2,2,64,2176]{3,2,0,1:T(8,128)(2,1)}, bf16[2,2,64,2176]{3,2,0,1:T(8,128)(2,1)}, u32[]{:S(2)}, u32[]{:S(2)}) collective-permute-start(bf16[2,2,64,2176]{3,2,0,1:T(8,128)(2,1)} %copy.59), channel_id=1, source_target_pairs={{0,8},{8,0},{16,24},{24,16},{1,9},{9,1},{17,25},{25,17},{2,10},{10... | collective-permute-start | bytes 3342344 | tf_op jit(solution)/shard_map/ppermute | solution.py:299
  334.1 19.7 %collective-permute-start.22 = (bf16[2,64,2176]{2,1,0:T(8,128)(2,1)}, bf16[2,64,2176]{2,1,0:T(8,128)(2,1)}, u32[]{:S(2)}, u32[]{:S(2)}) collective-permute-start(bf16[2,64,2176]{2,1,0:T(8,128)(2,1)} %get-tuple-element.81), channel_id=1, source_target_pairs={{0,16},{8,24},{16,0},{24,8},{1,17},{9,25},{17,1},{25,9},{2,18},{10... | collective-permute-start | bytes 1671176 | tf_op jit(solution)/shard_map/ppermute | solution.py:287
  350.8 18.8 %collective-permute-start.24 = (bf16[2,2,64,2176]{3,2,0,1:T(8,128)(2,1)}, bf16[2,2,64,2176]{3,2,0,1:T(8,128)(2,1)S(1)}, u32[]{:S(2)}, u32[]{:S(2)}) collective-permute-start(bf16[2,2,64,2176]{3,2,0,1:T(8,128)(2,1)} %copy.62), channel_id=1, source_target_pairs={{0,8},{8,0},{16,24},{24,16},{1,9},{9,1},{17,25},{25,17},{2,10},{10... | collective-permute-start | bytes 3342344 | tf_op jit(solution)/shard_map/ppermute | solution.py:299
  353.3 18.1 %collective-permute-start.23 = (bf16[2,64,2176]{2,1,0:T(8,128)(2,1)}, bf16[2,64,2176]{2,1,0:T(8,128)(2,1)}, u32[]{:S(2)}, u32[]{:S(2)}) collective-permute-start(bf16[2,64,2176]{2,1,0:T(8,128)(2,1)} %get-tuple-element.84), channel_id=1, source_target_pairs={{0,16},{8,24},{16,0},{24,8},{1,17},{9,25},{17,1},{25,9},{2,18},{10... | collective-permute-start | bytes 1671176 | tf_op jit(solution)/shard_map/ppermute | solution.py:287
  372.7 23.9 %collective-permute-start.27 = (bf16[2,64,2176]{2,1,0:T(8,128)(2,1)S(1)}, bf16[2,64,2176]{2,1,0:T(8,128)(2,1)S(1)}, u32[]{:S(2)}, u32[]{:S(2)}) collective-permute-start(bf16[2,64,2176]{2,1,0:T(8,128)(2,1)S(1)} %fusion.13), channel_id=1, source_target_pairs={{0,16},{8,24},{16,0},{24,8},{1,17},{9,25},{17,1},{25,9},{2,18},{10... | collective-permute-start | bytes 1671176 | tf_op jit(solution)/shard_map/ppermute | solution.py:287
  (16 other events, 87.0 us)

commit v5 on v3

--- a/solution.py
+++ b/solution.py
@@ -112,7 +112,7 @@
     left = slots_ref[0, :, :depth]
 
     def kern(near_slot):
-        marks = marks_ref[spots_ref[cluster * near_count + near_slot]]
+        marks = marks_ref[spots_ref[cluster * near_count + near_slot] - base]
         scores = lax.dot_general(
             left, marks, (((1,), (1,)), ((), ())), preferred_element_type=jnp.float32
         )
@@ -148,6 +148,7 @@
     slot_count = slots.shape[1]
     width = near_count * mark_count + slots.shape[2] - depth
     rows = mark_count // (2 * parts)
+    window = marks.shape[0] - slots.shape[0] + clusters
     shape = jax.ShapeDtypeStruct((clusters, parts, rows, width), jnp.bfloat16)
     spec = pl.BlockSpec((1, parts, rows, width), lambda a: (a, 0, 0, 0))
     return pl.pallas_call(
@@ -156,7 +157,11 @@
         in_specs=[
             pl.BlockSpec(memory_space=pltpu.SMEM),
             pl.BlockSpec((1, slot_count, slots.shape[2]), lambda a: (a + base, 0, 0)),
-            pl.BlockSpec(marks.shape, lambda a: (0, 0, 0), pipeline_mode=pl.Buffered(1)),
+            pl.BlockSpec(
+                tuple(pl.Element(size) for size in (window, mark_count, depth)),
+                lambda a: (base, 0, 0),
+                pipeline_mode=pl.Buffered(1),
+            ),
         ],
         out_specs=[spec, spec],
         out_shape=[shape, shape],

time: 398 us -> 387 us (0.972)
  Pallas kernels: 137 us -> 126 us
    pallas_call x8, Pallas kernels: 114 us -> 104 us  [blocks(): pl.pallas_call(functools.partial(block_kernel, base, near_count, scale),...]
  transfers between devices with their start and end apart: 22 -> 22, of which waited for: 9 -> 9; matrix products, arithmetic and copies ran while one was open for 9% -> 9% of each run, Pallas kernels for 22% -> 20%
where the time goes in v5:
time: 387 us; the launch traced here: 383 us
  waiting for transfers between devices  166 us (43%)
  Pallas kernels  126 us (33%)
  other arithmetic  33.4 us (9%)
  local copies, waits for them, and re-layouts  23.9 us (6%)
  starting transfers between devices  18.3 us (5%)
  between operations  14.8 us (4%)
    pallas_call x8, Pallas kernels, blocks(): pl.pallas_call(functools.partial(block_kernel, base, near_count, scale),...  104 us
    all_gather x1, waiting for transfers between devices, on_device(): all_rows = lax.all_gather(jnp.concatenate([rows, listed], axis=0), 'lmk')  62.2 us
    ppermute x3, waiting for transfers between devices, on_device(): piece = lax.ppermute(rims, 'cmp', swap) if turn else rims  44.5 us
    ppermute x1, waiting for transfers between devices, on_device(): low = lax.ppermute(quarter[owned - rim:], 'lmk', forward)  28.5 us
    ppermute x8, waiting for transfers between devices, cross(): pieces.append(lax.ppermute(sums[hop], 'cmp', across))  23.8 us
    pallas_call x1, Pallas kernels, dispatch(): pl.pallas_call(functools.partial(dispatch_kernel, cluster_count), grid=(s...  22.6 us
    unnamed x18, local copies, waits for them, and re-layouts  14.2 us
    convert_element_type x7, other arithmetic, on_device(): sums.append(mine.astype(jnp.bfloat16) if hop else mine)  12.5 us
  transfers between devices with their start and end apart: 22, of which 9 were waited for; matrix products, arithmetic and copies ran while one was open for 9% of the time, Pallas kernels for 20%

profile of v5, /device:TPU:0, one launch (start us, length us, event | category | flops | bytes accessed | tf_op | source)
XLA Modules:
  0.0 382.8 jit_solution(15537017445863661578)
XLA Ops:
  11.2 3.2 fusion
  17.7 3.0 collective-permute-start
  20.7 3.1 collective-permute-start.1
  23.8 28.5 %collective-permute-done = bf16[8,64,512]{2,1,0:T(8,128)(2,1)S(1)} collective-permute-done((bf16[8,64,512]{2,1,0:T(8,128)(2,1)S(1)}, bf16[8,64,512]{2,1,0:T(8,128)(2,1)S(1)}, u32[]{:S(2)}, u32[]{:S(2)}) %collective-permute-start) | collective-permute-done | bytes 524320 | tf_op jit(solution)/shard_map/ppermute | solution.py:206
  52.4 4.0 %collective-permute-done.1 = bf16[8,64,512]{2,1,0:T(8,128)(2,1)S(1)} collective-permute-done((bf16[8,64,512]{2,1,0:T(8,128)(2,1)S(1)}, bf16[8,64,512]{2,1,0:T(8,128)(2,1)S(1)}, u32[]{:S(2)}, u32[]{:S(2)}) %collective-permute-start.1) | collective-permute-done | bytes 524320 | tf_op jit(solution)/shard_map/ppermute | solution.py:207
  59.5 23.1 %collective-permute-done.3 = bf16[16,64,512]{2,1,0:T(8,128)(2,1)S(1)} collective-permute-done((bf16[16,64,512]{2,1,0:T(8,128)(2,1)S(1)}, bf16[16,64,512]{2,1,0:T(8,128)(2,1)S(1)}, u32[]{:S(2)}, u32[]{:S(2)}) %collective-permute-start.3) | collective-permute-done | bytes 1048608 | tf_op jit(solution)/shard_map/ppermute | solution.py:212
  82.6 21.5 %collective-permute-done.4 = bf16[16,64,512]{2,1,0:T(8,128)(2,1)S(1)} collective-permute-done((bf16[16,64,512]{2,1,0:T(8,128)(2,1)S(1)}, bf16[16,64,512]{2,1,0:T(8,128)(2,1)S(1)}, u32[]{:S(2)}, u32[]{:S(2)}) %collective-permute-start.4) | collective-permute-done | bytes 1048608 | tf_op jit(solution)/shard_map/ppermute | solution.py:212
  106.4 8.6 %pad_maximum_fusion.marks_ref = bf16[32,256,640]{2,1,0:T(8,128)(2,1)} fusion(bf16[32,256,128]{2,1,0:T(8,128)(2,1)S(1)} %broadcast_in_dim.47, bf16[8,256,512]{2,1,0:T(8,128)(2,1)S(1)} %bitcast.95, bf16[16,256,512]{2,1,0:T(8,128)(2,1)S(1)} %copy-done.1, bf16[8,256,512]{2,1,0:T(8,128)(2,1)S(1)} %bitcast.94), kind=kLoop, calls=%fused_computation.2 | loop fusion | flops 41943040 | bytes 20971520 | tf_op jit(solution)/shard_map/concatenate | solution.py:224
  115.0 62.2 %all-gather.3.cloned.1.call-done = bf16[8320,640]{1,0:T(8,128)(2,1)} async-done(((bf16[1040,640]{1,0:T(8,128)(2,1)}), bf16[8320,640]{1,0:T(8,128)(2,1)}) %all-gather.3.cloned.1.call-update) | async-done | bytes 10649616 | tf_op jit(solution)/shard_map/all_gather | solution.py:197
  178.2 22.6 %shard_map.68 = bf16[16,8,64,768]{3,2,1,0:T(8,128)(2,1)} custom-call(s32[1]{0:T(128)} %bitcast.1.first_ref, s32[8,4,1024]{2,1,0:T(4,128)S(1)} %slice_convert_fusion.lists_ref, bf16[8,1040,640]{2,1,0:T(8,128)(2,1)} %bitcast.97), custom_call_target="tpu_custom_call" | custom-call | flops 12884901888 | bytes 23068672 | tf_op jit(solution)/shard_map/pallas_call | solution.py:81
  200.8 12.9 %shard_map.70 = (bf16[2,2,64,2176]{3,2,1,0:T(8,128)(2,1)S(1)}, bf16[2,2,64,2176]{3,2,1,0:T(8,128)(2,1)S(1)}) custom-call(s32[129]{0:T(256)S(1)} %pad_add_fusion.spots_ref, bf16[16,512,768]{2,1,0:T(8,128)(2,1)} %bitcast.84, bf16[32,256,640]{2,1,0:T(8,128)(2,1)} %pad_maximum_fusion.marks_ref), custom_call_target="tpu_custom_call" | custom-call | flops 1048576 | bytes 1048576 | tf_op jit(solution)/shard_map/pallas_call | solution.py:154
  213.7 12.9 %shard_map.69 = (bf16[2,2,64,2176]{3,2,1,0:T(8,128)(2,1)S(1)}, bf16[2,2,64,2176]{3,2,1,0:T(8,128)(2,1)S(1)}) custom-call(s32[129]{0:T(256)S(1)} %pad_add_fusion.spots_ref, bf16[16,512,768]{2,1,0:T(8,128)(2,1)} %bitcast.85, bf16[32,256,640]{2,1,0:T(8,128)(2,1)} %pad_maximum_fusion.marks_ref), custom_call_target="tpu_custom_call" | custom-call | flops 1048576 | bytes 1048576 | tf_op jit(solution)/shard_map/pallas_call | solution.py:154
  231.5 3.4 fusion.6
  236.4 13.0 %shard_map.71 = (bf16[2,2,64,2176]{3,2,1,0:T(8,128)(2,1)S(1)}, bf16[2,2,64,2176]{3,2,1,0:T(8,128)(2,1)S(1)}) custom-call(s32[129]{0:T(256)S(1)} %pad_add_fusion.spots_ref, bf16[16,512,768]{2,1,0:T(8,128)(2,1)} %bitcast.86, bf16[32,256,640]{2,1,0:T(8,128)(2,1)} %pad_maximum_fusion.marks_ref), custom_call_target="tpu_custom_call" | custom-call | flops 1048576 | bytes 1048576 | tf_op jit(solution)/shard_map/pallas_call | solution.py:154
  251.1 12.9 %shard_map.72 = (bf16[2,2,64,2176]{3,2,1,0:T(8,128)(2,1)S(1)}, bf16[2,2,64,2176]{3,2,1,0:T(8,128)(2,1)S(1)}) custom-call(s32[129]{0:T(256)S(1)} %pad_add_fusion.spots_ref, bf16[16,512,768]{2,1,0:T(8,128)(2,1)} %bitcast.87, bf16[32,256,640]{2,1,0:T(8,128)(2,1)} %pad_maximum_fusion.marks_ref), custom_call_target="tpu_custom_call" | custom-call | flops 1048576 | bytes 1048576 | tf_op jit(solution)/shard_map/pallas_call | solution.py:154
  266.4 2.4 fusion.8
  270.3 12.9 %shard_map.73 = (bf16[2,2,64,2176]{3,2,1,0:T(8,128)(2,1)S(1)}, bf16[2,2,64,2176]{3,2,1,0:T(8,128)(2,1)S(1)}) custom-call(s32[129]{0:T(256)S(1)} %pad_add_fusion.spots_ref, bf16[16,512,768]{2,1,0:T(8,128)(2,1)} %bitcast.88, bf16[32,256,640]{2,1,0:T(8,128)(2,1)} %pad_maximum_fusion.marks_ref), custom_call_target="tpu_custom_call" | custom-call | flops 1048576 | bytes 1048576 | tf_op jit(solution)/shard_map/pallas_call | solution.py:154
  286.6 13.1 %shard_map.74 = (bf16[2,2,64,2176]{3,2,1,0:T(8,128)(2,1)S(1)}, bf16[2,2,64,2176]{3,2,1,0:T(8,128)(2,1)S(1)}) custom-call(s32[129]{0:T(256)S(1)} %pad_add_fusion.spots_ref, bf16[16,512,768]{2,1,0:T(8,128)(2,1)} %bitcast.89, bf16[32,256,640]{2,1,0:T(8,128)(2,1)} %pad_maximum_fusion.marks_ref), custom_call_target="tpu_custom_call" | custom-call | flops 1048576 | bytes 1048576 | tf_op jit(solution)/shard_map/pallas_call | solution.py:154
  306.1 12.9 %shard_map.75 = (bf16[2,2,64,2176]{3,2,1,0:T(8,128)(2,1)S(1)}, bf16[2,2,64,2176]{3,2,1,0:T(8,128)(2,1)S(1)}) custom-call(s32[129]{0:T(256)S(1)} %pad_add_fusion.spots_ref, bf16[16,512,768]{2,1,0:T(8,128)(2,1)} %bitcast.90, bf16[32,256,640]{2,1,0:T(8,128)(2,1)} %pad_maximum_fusion.marks_ref), custom_call_target="tpu_custom_call" | custom-call | flops 1048576 | bytes 1048576 | tf_op jit(solution)/shard_map/pallas_call | solution.py:154
  323.1 13.1 %shard_map.76 = (bf16[2,2,64,2176]{3,2,1,0:T(8,128)(2,1)S(1)}, bf16[2,2,64,2176]{3,2,1,0:T(8,128)(2,1)S(1)}) custom-call(s32[129]{0:T(256)S(1)} %pad_add_fusion.spots_ref, bf16[16,512,768]{2,1,0:T(8,128)(2,1)} %bitcast.91, bf16[32,256,640]{2,1,0:T(8,128)(2,1)} %pad_maximum_fusion.marks_ref), custom_call_target="tpu_custom_call" | custom-call | flops 1048576 | bytes 1048576 | tf_op jit(solution)/shard_map/pallas_call | solution.py:154
  340.7 12.6 %collective-permute-done.18 = bf16[2,64,2176]{2,1,0:T(8,128)(2,1)S(1)} collective-permute-done((bf16[2,64,2176]{2,1,0:T(8,128)(2,1)S(1)}, bf16[2,64,2176]{2,1,0:T(8,128)(2,1)S(1)}, u32[]{:S(2)}, u32[]{:S(2)}) %collective-permute-start.18) | collective-permute-done | bytes 557088 | tf_op jit(solution)/shard_map/ppermute | solution.py:247
  353.5 11.1 %collective-permute-done.20 = bf16[2,64,2176]{2,1,0:T(8,128)(2,1)S(1)} collective-permute-done((bf16[2,64,2176]{2,1,0:T(8,128)(2,1)S(1)}, bf16[2,64,2176]{2,1,0:T(8,128)(2,1)S(1)}, u32[]{:S(2)}, u32[]{:S(2)}) %collective-permute-start.20) | collective-permute-done | bytes 557088 | tf_op jit(solution)/shard_map/ppermute | solution.py:247
  366.1 4.1 %copy.68 = f32[128,8,8,256]{3,2,1,0:T(8,128)S(1)} copy(f32[128,8,8,256]{3,1,2,0:T(8,128)S(1)} %bitcast.92) | data formatting | bytes 16777216
  370.2 4.4 %copy.65 = f32[64,16,8,256]{3,2,1,0:T(8,128)} copy(f32[64,16,8,256]{3,2,0,1:T(8,128)S(1)} %bitcast.93) | data formatting | bytes 16777216
  (100 shorter events, 46.4 us)
Async XLA Ops:
  7.2 170.0 %all-gather.3.cloned.1.call-start = ((), (), s32[]{:S(2)}) async-start(), calls=%async_computation | async-start | bytes 11980800 | tf_op jit(solution)/shard_map/all_gather | solution.py:197
  11.2 3.5 copy-start.2
  17.7 40.4 %copy-start.6 = (s32[128,8]{0,1:T(8,128)S(1)}, s32[128,8]{0,1:T(8,128)}, u32[]{:S(2)}) copy-start(s32[128,8]{0,1:T(8,128)} %param.9) | copy-start | bytes 12292
  17.7 34.7 %collective-permute-start = (bf16[8,64,512]{2,1,0:T(8,128)(2,1)S(1)}, bf16[8,64,512]{2,1,0:T(8,128)(2,1)S(1)}, u32[]{:S(2)}, u32[]{:S(2)}) collective-permute-start(bf16[8,64,512]{2,1,0:T(8,128)(2,1)S(1)} %get-tuple-element.97), channel_id=1, source_target_pairs={{0,1},{1,2},{2,3},{3,4},{4,5},{5,6},{6,7},{7,0},{8,9},{9,10},{10,1... | collective-permute-start | bytes 1572872 | tf_op jit(solution)/shard_map/ppermute | solution.py:206
  20.7 35.7 %collective-permute-start.1 = (bf16[8,64,512]{2,1,0:T(8,128)(2,1)S(1)}, bf16[8,64,512]{2,1,0:T(8,128)(2,1)S(1)}, u32[]{:S(2)}, u32[]{:S(2)}) collective-permute-start(bf16[8,64,512]{2,1,0:T(8,128)(2,1)S(1)} %get-tuple-element.96), channel_id=1, source_target_pairs={{1,0},{2,1},{3,2},{4,3},{5,4},{6,5},{7,6},{0,7},{9,8},{10,9},{11,1... | collective-permute-start | bytes 1572872 | tf_op jit(solution)/shard_map/ppermute | solution.py:207
  56.4 2.9 collective-permute-start.2
  56.5 26.0 %collective-permute-start.3 = (bf16[16,64,512]{2,1,0:T(8,128)(2,1)S(1)}, bf16[16,64,512]{2,1,0:T(8,128)(2,1)S(1)}, u32[]{:S(2)}, u32[]{:S(2)}) collective-permute-start(bf16[16,64,512]{2,1,0:T(8,128)(2,1)S(1)} %constant_dynamic-update-slice_fusion), channel_id=1, source_target_pairs={{0,16},{8,24},{16,0},{24,8},{1,17},{9,25},{17,1},{25,9},{2,18},{10... | collective-permute-start | bytes 3145736 | tf_op jit(solution)/shard_map/ppermute | solution.py:212
  58.3 45.8 %collective-permute-start.4 = (bf16[16,64,512]{2,1,0:T(8,128)(2,1)S(1)}, bf16[16,64,512]{2,1,0:T(8,128)(2,1)S(1)}, u32[]{:S(2)}, u32[]{:S(2)}) collective-permute-start(bf16[16,64,512]{2,1,0:T(8,128)(2,1)S(1)} %constant_dynamic-update-slice_fusion), channel_id=1, source_target_pairs={{0,24},{8,16},{16,8},{24,0},{1,25},{9,17},{17,9},{25,1},{2,26},{10... | collective-permute-start | bytes 3145736 | tf_op jit(solution)/shard_map/ppermute | solution.py:212
  226.7 3.0 collective-permute-start.6
  227.9 3.6 collective-permute-start.5
  234.9 16.2 %collective-permute-start.7 = (bf16[2,64,2176]{2,1,0:T(8,128)(2,1)S(1)}, bf16[2,64,2176]{2,1,0:T(8,128)(2,1)}, u32[]{:S(2)}, u32[]{:S(2)}) collective-permute-start(bf16[2,64,2176]{2,1,0:T(8,128)(2,1)S(1)} %get-tuple-element.53), channel_id=1, source_target_pairs={{0,16},{8,24},{16,0},{24,8},{1,17},{9,25},{17,1},{25,9},{2,18},{10... | collective-permute-start | bytes 1671176 | tf_op jit(solution)/shard_map/ppermute | solution.py:247
  250.5 15.9 %collective-permute-start.8 = (bf16[2,2,64,2176]{3,2,0,1:T(8,128)(2,1)}, bf16[2,2,64,2176]{3,2,0,1:T(8,128)(2,1)}, u32[]{:S(2)}, u32[]{:S(2)}) collective-permute-start(bf16[2,2,64,2176]{3,2,0,1:T(8,128)(2,1)} %copy.49), channel_id=1, source_target_pairs={{0,8},{8,0},{16,24},{24,16},{1,9},{9,1},{17,25},{25,17},{2,10},{10... | collective-permute-start | bytes 3342344 | tf_op jit(solution)/shard_map/ppermute | solution.py:259
  250.5 18.3 %collective-permute-start.9 = (bf16[2,64,2176]{2,1,0:T(8,128)(2,1)}, bf16[2,64,2176]{2,1,0:T(8,128)(2,1)S(1)}, u32[]{:S(2)}, u32[]{:S(2)}) collective-permute-start(bf16[2,64,2176]{2,1,0:T(8,128)(2,1)} %get-tuple-element.60), channel_id=1, source_target_pairs={{0,16},{8,24},{16,0},{24,8},{1,17},{9,25},{17,1},{25,9},{2,18},{10... | collective-permute-start | bytes 1671176 | tf_op jit(solution)/shard_map/ppermute | solution.py:247
  264.1 20.3 %collective-permute-start.10 = (bf16[2,2,64,2176]{3,2,0,1:T(8,128)(2,1)S(1)}, bf16[2,2,64,2176]{3,2,0,1:T(8,128)(2,1)}, u32[]{:S(2)}, u32[]{:S(2)}) collective-permute-start(bf16[2,2,64,2176]{3,2,0,1:T(8,128)(2,1)S(1)} %copy.52), channel_id=1, source_target_pairs={{0,8},{8,0},{16,24},{24,16},{1,9},{9,1},{17,25},{25,17},{2,10},{10... | collective-permute-start | bytes 3342344 | tf_op jit(solution)/shard_map/ppermute | solution.py:259
  268.8 17.8 %collective-permute-start.11 = (bf16[2,64,2176]{2,1,0:T(8,128)(2,1)}, bf16[2,64,2176]{2,1,0:T(8,128)(2,1)}, u32[]{:S(2)}, u32[]{:S(2)}) collective-permute-start(bf16[2,64,2176]{2,1,0:T(8,128)(2,1)} %get-tuple-element.67), channel_id=1, source_target_pairs={{0,16},{8,24},{16,0},{24,8},{1,17},{9,25},{17,1},{25,9},{2,18},{10... | collective-permute-start | bytes 1671176 | tf_op jit(solution)/shard_map/ppermute | solution.py:247
  284.3 17.9 %collective-permute-start.12 = (bf16[2,2,64,2176]{3,2,0,1:T(8,128)(2,1)}, bf16[2,2,64,2176]{3,2,0,1:T(8,128)(2,1)}, u32[]{:S(2)}, u32[]{:S(2)}) collective-permute-start(bf16[2,2,64,2176]{3,2,0,1:T(8,128)(2,1)} %copy.55), channel_id=1, source_target_pairs={{0,8},{8,0},{16,24},{24,16},{1,9},{9,1},{17,25},{25,17},{2,10},{10... | collective-permute-start | bytes 3342344 | tf_op jit(solution)/shard_map/ppermute | solution.py:259
  286.0 18.6 %collective-permute-start.13 = (bf16[2,64,2176]{2,1,0:T(8,128)(2,1)S(1)}, bf16[2,64,2176]{2,1,0:T(8,128)(2,1)S(1)}, u32[]{:S(2)}, u32[]{:S(2)}) collective-permute-start(bf16[2,64,2176]{2,1,0:T(8,128)(2,1)S(1)} %get-tuple-element.74), channel_id=1, source_target_pairs={{0,16},{8,24},{16,0},{24,8},{1,17},{9,25},{17,1},{25,9},{2,18},{10... | collective-permute-start | bytes 1671176 | tf_op jit(solution)/shard_map/ppermute | solution.py:247
  300.8 19.4 %collective-permute-start.14 = (bf16[2,2,64,2176]{3,2,0,1:T(8,128)(2,1)}, bf16[2,2,64,2176]{3,2,0,1:T(8,128)(2,1)}, u32[]{:S(2)}, u32[]{:S(2)}) collective-permute-start(bf16[2,2,64,2176]{3,2,0,1:T(8,128)(2,1)} %copy.58), channel_id=1, source_target_pairs={{0,8},{8,0},{16,24},{24,16},{1,9},{9,1},{17,25},{25,17},{2,10},{10... | collective-permute-start | bytes 3342344 | tf_op jit(solution)/shard_map/ppermute | solution.py:259
  304.6 18.5 %collective-permute-start.15 = (bf16[2,64,2176]{2,1,0:T(8,128)(2,1)}, bf16[2,64,2176]{2,1,0:T(8,128)(2,1)}, u32[]{:S(2)}, u32[]{:S(2)}) collective-permute-start(bf16[2,64,2176]{2,1,0:T(8,128)(2,1)} %get-tuple-element.81), channel_id=1, source_target_pairs={{0,16},{8,24},{16,0},{24,8},{1,17},{9,25},{17,1},{25,9},{2,18},{10... | collective-permute-start | bytes 1671176 | tf_op jit(solution)/shard_map/ppermute | solution.py:247
  320.0 17.7 %collective-permute-start.17 = (bf16[2,2,64,2176]{3,2,0,1:T(8,128)(2,1)}, bf16[2,2,64,2176]{3,2,0,1:T(8,128)(2,1)S(1)}, u32[]{:S(2)}, u32[]{:S(2)}) collective-permute-start(bf16[2,2,64,2176]{3,2,0,1:T(8,128)(2,1)} %copy.61), channel_id=1, source_target_pairs={{0,8},{8,0},{16,24},{24,16},{1,9},{9,1},{17,25},{25,17},{2,10},{10... | collective-permute-start | bytes 3342344 | tf_op jit(solution)/shard_map/ppermute | solution.py:259
  322.5 16.9 %collective-permute-start.16 = (bf16[2,64,2176]{2,1,0:T(8,128)(2,1)}, bf16[2,64,2176]{2,1,0:T(8,128)(2,1)S(1)}, u32[]{:S(2)}, u32[]{:S(2)}) collective-permute-start(bf16[2,64,2176]{2,1,0:T(8,128)(2,1)} %get-tuple-element.84), channel_id=1, source_target_pairs={{0,16},{8,24},{16,0},{24,8},{1,17},{9,25},{17,1},{25,9},{2,18},{10... | collective-permute-start | bytes 1671176 | tf_op jit(solution)/shard_map/ppermute | solution.py:247
  336.2 3.3 collective-permute-start.19
  337.8 15.5 %collective-permute-start.18 = (bf16[2,64,2176]{2,1,0:T(8,128)(2,1)S(1)}, bf16[2,64,2176]{2,1,0:T(8,128)(2,1)S(1)}, u32[]{:S(2)}, u32[]{:S(2)}) collective-permute-start(bf16[2,64,2176]{2,1,0:T(8,128)(2,1)S(1)} %fusion.12), channel_id=1, source_target_pairs={{0,16},{8,24},{16,0},{24,8},{1,17},{9,25},{17,1},{25,9},{2,18},{10... | collective-permute-start | bytes 1671176 | tf_op jit(solution)/shard_map/ppermute | solution.py:247
  339.6 25.0 %collective-permute-start.20 = (bf16[2,64,2176]{2,1,0:T(8,128)(2,1)S(1)}, bf16[2,64,2176]{2,1,0:T(8,128)(2,1)S(1)}, u32[]{:S(2)}, u32[]{:S(2)}) collective-permute-start(bf16[2,64,2176]{2,1,0:T(8,128)(2,1)S(1)} %fusion.13), channel_id=1, source_target_pairs={{0,16},{8,24},{16,0},{24,8},{1,17},{9,25},{17,1},{25,9},{2,18},{10... | collective-permute-start | bytes 1671176 | tf_op jit(solution)/shard_map/ppermute | solution.py:247
  (5 other events, 9.1 us)
Sparse Core Ops, SparseCore 0:
  11.3 165.8 all-gather.2
